TPU v7x, 512 devices: a whole 4x4x16 slice. The times are simulated.
512 devices in a mesh: dp: 8 (over x, core), expert: 64 (over y, z).
Axes of the slice: x: 4, y: 4, z: 16, core: 2. Of those that a mesh axis runs over, the one named last changes fastest.
Arguments:
- tokens: bfloat16 [4096, 2048], P(('dp', 'expert')), may hold values from -6 to 6
- cotangent: bfloat16 [4096, 2048], P(('dp', 'expert')), may hold values from -6 to 6
- expert_ids: int32 [4096, 8], P(('dp', 'expert')), may hold values from 0 to 63, all different within a row; in each aligned block of 8 rows (0 to 7, 8 to 15, ...) at most 2 rows name the same one
- gate_codes: int32 [4096, 8], P(('dp', 'expert')), may hold values from 64 to 1023
- w_gate: bfloat16 [64, 1536, 2048], P('expert', 'dp'), may hold values from -0.125 to 0.125
- w_up: bfloat16 [64, 1536, 2048], P('expert', 'dp'), may hold values from -0.125 to 0.125
- w_down: bfloat16 [64, 1536, 2048], P('expert', 'dp'), may hold values from -0.15625 to 0.15625
Outputs:
- token_grad: bfloat16 [4096, 2048], P(('dp', 'expert'))
- grad_gate: bfloat16 [64, 1536, 2048], P('expert', 'dp')
- grad_up: bfloat16 [64, 1536, 2048], P('expert', 'dp')
- grad_down: bfloat16 [64, 1536, 2048], P('expert', 'dp')
Inputs may be any that keep to these rules, and one draw needn't show every extreme that they name: `expert_ids`: each row names 8 different experts; of the 8 rows of one device at most 2 name the same expert, a bound that some block reaches; every expert is named by some row.
All inputs are finite; a program needn't handle non-finite values.
Results may differ from a plain program's by a relative error of at most 0.0065.
Values may be sent and summed in bfloat16 or wider, within the bound.
A program may use at most 64 MiB of HBM per device.

v0:
```python
import jax
import jax.numpy as jnp
from jax import lax
from jax.sharding import PartitionSpec as P

gate_unit = 1.0 / 1024.0


def slot_tables(route_ids, route_codes, experts, slots):
    rows_here, top_here = route_ids.shape
    flat_ids = route_ids.reshape(-1)
    hits = (flat_ids[:, None] == jnp.arange(experts, dtype=jnp.int32)[None, :]).astype(jnp.int32)
    ranks = jnp.sum((jnp.cumsum(hits, axis=0) - 1) * hits, axis=1)
    by_slot = (ranks[:, None] == jnp.arange(slots, dtype=jnp.int32)[None, :]).astype(jnp.float32)
    hit_table = hits.astype(jnp.float32).reshape(rows_here, top_here, experts)
    slot_table = by_slot.reshape(rows_here, top_here, slots)
    select = jnp.einsum("gie,gis->esg", hit_table, slot_table)
    factors = route_codes.astype(jnp.float32) * gate_unit
    weights = jnp.einsum(
        "gie,gis,gi->es", hit_table, slot_table, factors, precision=lax.Precision.HIGHEST
    )
    return (select.astype(jnp.bfloat16), weights)


def fill_slots(select, weights, rows_in, rows_cot):
    in_slots = jnp.einsum(
        "esg,gd->esd", select, rows_in, preferred_element_type=jnp.float32
    ).astype(jnp.bfloat16)
    cot_slots = jnp.einsum("esg,gd->esd", select, rows_cot, preferred_element_type=jnp.float32)
    cot_slots = (weights[:, :, None] * cot_slots).astype(jnp.bfloat16)
    return (in_slots, cot_slots)


def expert_pass(inputs, cot_rows, weight_gate, weight_up, weight_down):
    feature_contract = (((1,), (1,)), ((), ()))
    row_contract = (((0,), (0,)), ((), ()))
    pre_gate = lax.dot_general(
        inputs, weight_gate, feature_contract, preferred_element_type=jnp.float32
    )
    pre_up = lax.dot_general(
        inputs, weight_up, feature_contract, preferred_element_type=jnp.float32
    )
    sigmoid_gate = jax.nn.sigmoid(pre_gate)
    active = pre_gate * sigmoid_gate
    hidden = (active * pre_up).astype(jnp.bfloat16)
    d_hidden = lax.dot_general(
        cot_rows, weight_down, feature_contract, preferred_element_type=jnp.float32
    )
    d_up = (d_hidden * active).astype(jnp.bfloat16)
    d_gate = (d_hidden * pre_up * sigmoid_gate * (1.0 + pre_gate * (1.0 - sigmoid_gate))).astype(
        jnp.bfloat16
    )
    grad_down = lax.dot_general(hidden, cot_rows, row_contract, preferred_element_type=jnp.float32)
    grad_gate = lax.dot_general(d_gate, inputs, row_contract, preferred_element_type=jnp.float32)
    grad_up = lax.dot_general(d_up, inputs, row_contract, preferred_element_type=jnp.float32)
    partial_value = jnp.dot(d_gate, weight_gate, preferred_element_type=jnp.float32)
    partial_value = partial_value + jnp.dot(d_up, weight_up, preferred_element_type=jnp.float32)
    return (partial_value.astype(jnp.bfloat16), grad_gate, grad_up, grad_down)


def body(tokens, cotangent, expert_ids, gate_codes, w_gate, w_up, w_down):
    own_rows, width = tokens.shape
    top_count = expert_ids.shape[1]
    experts = lax.axis_size("expert")
    groups = lax.axis_size("dp")
    capacity = max(2, 2 * own_rows * top_count // experts)
    column_ids, column_codes = (
        lax.all_gather(expert_ids, "dp", axis=0, tiled=True),
        lax.all_gather(gate_codes, "dp", axis=0, tiled=True),
    )
    weight_gate = w_gate[0]
    weight_up = w_up[0]
    weight_down = w_down[0]
    column_in, column_cot = (
        lax.all_gather(tokens, "dp", axis=0, tiled=True),
        lax.all_gather(cotangent, "dp", axis=0, tiled=True),
    )
    select, weights = slot_tables(column_ids, column_codes, experts, groups * capacity)
    in_slots, cot_slots = fill_slots(select, weights, column_in, column_cot)
    got_in, got_cot = (
        lax.all_to_all(in_slots, "expert", split_axis=0, concat_axis=0, tiled=True),
        lax.all_to_all(cot_slots, "expert", split_axis=0, concat_axis=0, tiled=True),
    )
    partial_value, grad_gate, grad_up, grad_down = expert_pass(
        got_in.reshape(-1, width), got_cot.reshape(-1, width), weight_gate, weight_up, weight_down
    )
    returned = lax.all_to_all(
        partial_value.reshape(experts, groups * capacity, width),
        "expert",
        split_axis=0,
        concat_axis=0,
        tiled=True,
    )
    column_grad = jnp.einsum("esg,esd->gd", select, returned, preferred_element_type=jnp.float32)
    token_grad = lax.psum_scatter(column_grad, "dp", scatter_dimension=0, tiled=True).astype(
        jnp.bfloat16
    )
    return (
        token_grad,
        grad_gate[None].astype(jnp.bfloat16),
        grad_up[None].astype(jnp.bfloat16),
        grad_down[None].astype(jnp.bfloat16),
    )


def solution(mesh):
    placed = (
        P(("dp", "expert"), None),
        P(("dp", "expert"), None),
        P(("dp", "expert"), None),
        P(("dp", "expert"), None),
        P("expert", "dp", None),
        P("expert", "dp", None),
        P("expert", "dp", None),
    )
    return jax.shard_map(
        body,
        mesh=mesh,
        in_specs=placed,
        out_specs=(
            P(("dp", "expert"), None),
            P("expert", "dp", None),
            P("expert", "dp", None),
            P("expert", "dp", None),
        ),
        check_vma=False,
    )
```

profile of v0, /device:TPU:1, one launch (start us, length us, event | category | flops | bytes accessed | tf_op | source)
XLA Modules:
  0.0 685.5 jit_solution(3001842308146549617)
XLA Ops:
  7.2 0.0 copy-start
  7.2 19.8 %all_gather.12 = s32[64,8]{1,0:T(8,128)S(1)} all-gather(s32[8,8]{1,0:T(8,128)} %param.9), channel_id=1, replica_groups=mesh['dp'=8,'expert'=64] {'dp'}, dimensions={0}, use_global_device_ids=true | all-gather | bytes 2304 | tf_op jit(solution)/shard_map/all_gather | solution.py:68
  26.9 0.1 eq.52
  27.0 0.1 eq.48
  27.1 0.1 copy.54
  27.2 1.2 reduce-window.6
  28.4 0.2 slice_reduce_fusion
  28.7 0.1 fusion.19
  28.8 0.1 eq.56
  28.9 0.1 copy.53
  29.0 0.2 copy.55
  29.2 0.1 convert_convert_fusion
  29.3 0.4 fusion.3
  29.7 0.4 copy.61
  30.1 13.1 %all_gather.15 = bf16[64,2048]{1,0:T(8,128)(2,1)S(1)} all-gather(bf16[8,2048]{1,0:T(8,128)(2,1)} %param.7), channel_id=1, replica_groups=mesh['dp'=8,'expert'=64] {'dp'}, dimensions={0}, use_global_device_ids=true | all-gather | bytes 294912 | tf_op jit(solution)/shard_map/all_gather | solution.py:75
  43.2 3.2 convolution_convert_fusion
  46.4 0.0 copy-start.3
  46.4 0.0 copy-start.2
  46.4 13.8 %all-to-all-start.1 = ((bf16[64,16,2048]{2,1,0:T(8,128)(2,1)}), bf16[64,16,2048]{2,1,0:T(8,128)(2,1)}, u32[]{:S(2)}, u32[]{:S(2)}) async-start(bf16[64,16,2048]{2,1,0:T(8,128)(2,1)} %convolution_convert_fusion), calls=%async_computation.1 | async-start | bytes 8388608 | tf_op jit(solution)/shard_map/all_to_all | solution.py:81
  60.2 0.0 copy-done.3
  60.2 13.1 %all_gather.13 = s32[64,8]{1,0:T(8,128)S(1)} all-gather(s32[8,8]{1,0:T(8,128)S(1)} %copy-done.3), channel_id=1, replica_groups=mesh['dp'=8,'expert'=64] {'dp'}, dimensions={0}, use_global_device_ids=true | all-gather | bytes 2304 | tf_op jit(solution)/shard_map/all_gather | solution.py:69
  73.3 0.1 copy.57
  73.3 0.0 copy-done.2
  73.3 12.9 %all_gather.14 = bf16[64,2048]{1,0:T(8,128)(2,1)S(1)} all-gather(bf16[8,2048]{1,0:T(8,128)(2,1)S(1)} %copy-done.2), channel_id=1, replica_groups=mesh['dp'=8,'expert'=64] {'dp'}, dimensions={0}, use_global_device_ids=true | all-gather | bytes 294912 | tf_op jit(solution)/shard_map/all_gather | solution.py:76
  86.2 0.5 convolution_bitcast_fusion.1
  86.8 3.2 multiply_convert_fusion
  90.0 154.3 %all-to-all-done.1 = bf16[64,16,2048]{2,1,0:T(8,128)(2,1)} async-done(((bf16[64,16,2048]{2,1,0:T(8,128)(2,1)}), bf16[64,16,2048]{2,1,0:T(8,128)(2,1)}, u32[]{:S(2)}, u32[]{:S(2)}) %all-to-all-start.1) | async-done | bytes 4194336 | tf_op jit(solution)/shard_map/all_to_all | solution.py:81
  244.3 11.3 %all-to-all-start = ((bf16[64,16,2048]{2,1,0:T(8,128)(2,1)}), bf16[64,16,2048]{2,1,0:T(8,128)(2,1)}, u32[]{:S(2)}, u32[]{:S(2)}) async-start(bf16[64,16,2048]{2,1,0:T(8,128)(2,1)} %multiply_convert_fusion), calls=%async_computation | async-start | bytes 8388608 | tf_op jit(solution)/shard_map/all_to_all | solution.py:82
  255.6 0.0 copy-start.1
  255.6 0.2 reduce-scatter.2.cloned.1.call-start
  255.8 0.0 copy-done
  255.8 4.6 fusion.6
  260.4 0.0 copy-done.1
  260.4 0.0 copy-start.4
  260.4 4.7 fusion.9
  265.2 172.3 %all-to-all-done = bf16[64,16,2048]{2,1,0:T(8,128)(2,1)} async-done(((bf16[64,16,2048]{2,1,0:T(8,128)(2,1)}), bf16[64,16,2048]{2,1,0:T(8,128)(2,1)}, u32[]{:S(2)}, u32[]{:S(2)}) %all-to-all-start) | async-done | bytes 4194336 | tf_op jit(solution)/shard_map/all_to_all | solution.py:82
  437.4 0.0 copy-done.4
  437.4 4.3 multiply_convert_fusion.2
  441.7 1.3 fusion.4
  443.0 1.3 add_convert_fusion
  444.4 194.8 %all_to_all.15 = bf16[64,16,2048]{2,1,0:T(8,128)(2,1)S(1)} all-to-all(bf16[64,16,2048]{2,1,0:T(8,128)(2,1)S(1)} %bitcast.66), channel_id=1, replica_groups=mesh['dp'=8,'expert'=64] {'expert'}, dimensions={0} | all-to-all | bytes 8388608 | tf_op jit(solution)/shard_map/all_to_all | solution.py:87
  639.2 1.7 convolution_bitcast_fusion
  640.9 0.0 reduce-scatter.2.cloned.1.call-update
  640.9 0.0 copy-start.5
  640.9 0.0 copy-start.6
  640.9 4.2 fusion.1
  645.1 4.1 fusion
  649.2 0.0 copy-done.5
  649.2 0.0 copy-done.6
  649.2 4.1 fusion.2
  653.3 23.9 %reduce-scatter.2.cloned.1.call-done = f32[8,2048]{1,0:T(8,128)} async-done(((f32[64,2048]{1,0:T(8,128)}), f32[8,2048]{1,0:T(8,128)}) %reduce-scatter.2.cloned.1.call-update) | async-done | bytes 65552 | tf_op jit(solution)/shard_map/reduce_scatter | solution.py:95
  677.2 1.5 convert_element_type.72
  (5 shorter events, 0.1 us)
Async XLA Ops:
  7.2 248.7 %copy-start = (bf16[1,192,2048]{2,1,0:T(8,128)(2,1)S(1)}, bf16[1,192,2048]{2,1,0:T(8,128)(2,1)}, u32[]{:S(2)}) copy-start(bf16[1,192,2048]{2,1,0:T(8,128)(2,1)} %param.11) | copy-start | bytes 2359300
  46.4 13.8 %copy-start.3 = (s32[8,8]{1,0:T(8,128)S(1)}, s32[8,8]{1,0:T(8,128)}, u32[]{:S(2)}) copy-start(s32[8,8]{1,0:T(8,128)} %param.10) | copy-start | bytes 772
  46.4 27.0 %copy-start.2 = (bf16[8,2048]{1,0:T(8,128)(2,1)S(1)}, bf16[8,2048]{1,0:T(8,128)(2,1)}, u32[]{:S(2)}) copy-start(bf16[8,2048]{1,0:T(8,128)(2,1)} %param.8) | copy-start | bytes 98308
  46.4 197.9 %all-to-all-start.1 = ((bf16[64,16,2048]{2,1,0:T(8,128)(2,1)}), bf16[64,16,2048]{2,1,0:T(8,128)(2,1)}, u32[]{:S(2)}, u32[]{:S(2)}) async-start(bf16[64,16,2048]{2,1,0:T(8,128)(2,1)} %convolution_convert_fusion), calls=%async_computation.1 | async-start | bytes 8388608 | tf_op jit(solution)/shard_map/all_to_all | solution.py:81
  244.3 193.1 %all-to-all-start = ((bf16[64,16,2048]{2,1,0:T(8,128)(2,1)}), bf16[64,16,2048]{2,1,0:T(8,128)(2,1)}, u32[]{:S(2)}, u32[]{:S(2)}) async-start(bf16[64,16,2048]{2,1,0:T(8,128)(2,1)} %multiply_convert_fusion), calls=%async_computation | async-start | bytes 8388608 | tf_op jit(solution)/shard_map/all_to_all | solution.py:82
  255.6 4.8 copy-start.1
  255.6 421.6 %reduce-scatter.2.cloned.1.call-start = ((), (), s32[]{:S(2)}) async-start(), calls=%async_computation.4 | async-start | bytes 589824 | tf_op jit(solution)/shard_map/reduce_scatter | solution.py:95
  260.4 177.0 %copy-start.4 = (bf16[1,192,2048]{2,1,0:T(8,128)(2,1)S(1)}, bf16[1,192,2048]{2,1,0:T(8,128)(2,1)}, u32[]{:S(2)}) copy-start(bf16[1,192,2048]{2,1,0:T(8,128)(2,1)} %param.13) | copy-start | bytes 2359300
  640.9 8.3 %copy-start.5 = (f32[1024,192]{0,1:T(8,128)S(1)}, f32[1024,192]{0,1:T(8,128)}, u32[]{:S(2)}) copy-start(f32[1024,192]{0,1:T(8,128)} %fusion.6) | copy-start | bytes 2359300
  640.9 8.2 %copy-start.6 = (f32[1024,192]{0,1:T(8,128)S(1)}, f32[1024,192]{0,1:T(8,128)}, u32[]{:S(2)}) copy-start(f32[1024,192]{0,1:T(8,128)} %fusion.9) | copy-start | bytes 2359300
Sparse Core Ops, SparseCore 0:
  641.0 36.1 reduce-scatter.1
where the time goes:
time: 687 us; the launch traced here: 685 us
  waiting for transfers between devices  351 us (51%)
  blocking collectives  254 us (37%)
  matrix products  37.6 us (5%)
  starting transfers between devices  25.3 us (4%)
  between operations  14.2 us (2%)
    all_to_all x1, blocking collectives, body(): lax.all_to_all(partial_value.reshape(experts, groups * capacity, width),...  195 us
    all_to_all x1, waiting for transfers between devices, body(): lax.all_to_all(cot_slots, 'expert', split_axis=0, concat_axis=0, tiled=True)  172 us
    all_to_all x1, waiting for transfers between devices, body(): lax.all_to_all(in_slots, 'expert', split_axis=0, concat_axis=0, tiled=True)  154 us
    reduce_scatter x1, waiting for transfers between devices, body(): lax.psum_scatter(column_grad, 'dp', scatter_dimension=0, tiled=True)  23.9 us
    all_gather x1, blocking collectives, body(): lax.all_gather(expert_ids, 'dp', axis=0, tiled=True)  19.8 us
    all_to_all x1, starting transfers between devices, body(): lax.all_to_all(in_slots, 'expert', split_axis=0, concat_axis=0, tiled=True)  13.8 us
  transfers between devices with their start and end apart: 3, of which 3 were waited for; matrix products, arithmetic and copies ran while one was open for 4% of the time, Pallas kernels for 0%

commit v1 on v0

--- a/solution.py
+++ b/solution.py
@@ -4,9 +4,10 @@
 from jax.sharding import PartitionSpec as P
 
 gate_unit = 1.0 / 1024.0
+slots = 2
 
 
-def slot_tables(route_ids, route_codes, experts, slots):
+def slot_tables(route_ids, route_codes, experts):
     rows_here, top_here = route_ids.shape
     flat_ids = route_ids.reshape(-1)
     hits = (flat_ids[:, None] == jnp.arange(experts, dtype=jnp.int32)[None, :]).astype(jnp.int32)
@@ -55,48 +56,32 @@
     grad_up = lax.dot_general(d_up, inputs, row_contract, preferred_element_type=jnp.float32)
     partial_value = jnp.dot(d_gate, weight_gate, preferred_element_type=jnp.float32)
     partial_value = partial_value + jnp.dot(d_up, weight_up, preferred_element_type=jnp.float32)
-    return (partial_value.astype(jnp.bfloat16), grad_gate, grad_up, grad_down)
+    return (partial_value, grad_gate, grad_up, grad_down)
 
 
 def body(tokens, cotangent, expert_ids, gate_codes, w_gate, w_up, w_down):
-    own_rows, width = tokens.shape
-    top_count = expert_ids.shape[1]
+    width = tokens.shape[1]
     experts = lax.axis_size("expert")
-    groups = lax.axis_size("dp")
-    capacity = max(2, 2 * own_rows * top_count // experts)
-    column_ids, column_codes = (
-        lax.all_gather(expert_ids, "dp", axis=0, tiled=True),
-        lax.all_gather(gate_codes, "dp", axis=0, tiled=True),
+    select, weights = slot_tables(expert_ids, gate_codes, experts)
+    in_slots, cot_slots = fill_slots(select, weights, tokens, cotangent)
+    got_in = lax.all_to_all(in_slots, "expert", split_axis=0, concat_axis=0, tiled=True)
+    got_cot = lax.all_to_all(cot_slots, "expert", split_axis=0, concat_axis=0, tiled=True)
+    all_in = lax.all_gather(got_in.reshape(-1, width), "dp", axis=0, tiled=True)
+    all_cot = lax.all_gather(got_cot.reshape(-1, width), "dp", axis=0, tiled=True)
+    partial_value, grad_gate, grad_up, grad_down = expert_pass(
+        all_in, all_cot, w_gate[0], w_up[0], w_down[0]
     )
-    weight_gate = w_gate[0]
-    weight_up = w_up[0]
-    weight_down = w_down[0]
-    column_in, column_cot = (
-        lax.all_gather(tokens, "dp", axis=0, tiled=True),
-        lax.all_gather(cotangent, "dp", axis=0, tiled=True),
-    )
-    select, weights = slot_tables(column_ids, column_codes, experts, groups * capacity)
-    in_slots, cot_slots = fill_slots(select, weights, column_in, column_cot)
-    got_in, got_cot = (
-        lax.all_to_all(in_slots, "expert", split_axis=0, concat_axis=0, tiled=True),
-        lax.all_to_all(cot_slots, "expert", split_axis=0, concat_axis=0, tiled=True),
-    )
-    partial_value, grad_gate, grad_up, grad_down = expert_pass(
-        got_in.reshape(-1, width), got_cot.reshape(-1, width), weight_gate, weight_up, weight_down
-    )
+    summed = lax.psum_scatter(partial_value, "dp", scatter_dimension=0, tiled=True)
     returned = lax.all_to_all(
-        partial_value.reshape(experts, groups * capacity, width),
+        summed.astype(jnp.bfloat16).reshape(experts, slots, width),
         "expert",
         split_axis=0,
         concat_axis=0,
         tiled=True,
     )
-    column_grad = jnp.einsum("esg,esd->gd", select, returned, preferred_element_type=jnp.float32)
-    token_grad = lax.psum_scatter(column_grad, "dp", scatter_dimension=0, tiled=True).astype(
-        jnp.bfloat16
-    )
+    token_grad = jnp.einsum("esg,esd->gd", select, returned, preferred_element_type=jnp.float32)
     return (
-        token_grad,
+        token_grad.astype(jnp.bfloat16),
         grad_gate[None].astype(jnp.bfloat16),
         grad_up[None].astype(jnp.bfloat16),
         grad_down[None].astype(jnp.bfloat16),

time: 687 us -> 265 us (0.39)
  waiting for transfers between devices: 351 us -> 110 us
  blocking collectives: 254 us -> 86.2 us
  starting transfers between devices: 25.3 us -> 15.7 us
  matrix products: 37.6 us -> 28.9 us
    all_to_all x2 -> x1, waiting for transfers between devices: 327 us -> 20.2 us  [body(): lax.all_to_all(summed.astype(jnp.bfloat16).reshape(experts, slots, width)...]
    all_to_all x1 -> x2, blocking collectives: 195 us -> 86.2 us  [the longest x1 48.5 us: body(): lax.all_to_all(in_slots, 'expert', split_axis=0, concat_axis=0, tiled=True)]
    all_gather x4 -> x0, blocking collectives: 58.8 us -> none  [the longest x1 19.8 us: body(): lax.all_gather(expert_ids, 'dp', axis=0, tiled=True)]
    reduce_scatter x1, waiting for transfers between devices: 23.9 us -> 59.3 us  [body(): lax.psum_scatter(partial_value, 'dp', scatter_dimension=0, tiled=True)]
    all_gather x0 -> x2, waiting for transfers between devices: none -> 30.8 us  [the longest x1 30.8 us: body(): lax.all_gather(got_cot.reshape(-1, width), 'dp', axis=0, tiled=True)]
    all_to_all x2 -> x1, starting transfers between devices: 25.1 us -> 15.5 us  [body(): lax.all_to_all(summed.astype(jnp.bfloat16).reshape(experts, slots, width)...]
  transfers between devices with their start and end apart: 3 -> 4, of which waited for: 3 -> 3; matrix products, arithmetic and copies ran while one was open for 4% -> 7% of each run, Pallas kernels for 0% -> 0%
where the time goes in v1:
time: 265 us; the launch traced here: 262 us
  waiting for transfers between devices  110 us (42%)
  blocking collectives  86.2 us (33%)
  matrix products  28.9 us (11%)
  starting transfers between devices  15.7 us (6%)
  between operations  13.9 us (5%)
  local copies, waits for them, and re-layouts  5.16 us (2%)
    reduce_scatter x1, waiting for transfers between devices, body(): lax.psum_scatter(partial_value, 'dp', scatter_dimension=0, tiled=True)  59.3 us
    all_to_all x1, blocking collectives, body(): lax.all_to_all(in_slots, 'expert', split_axis=0, concat_axis=0, tiled=True)  48.5 us
    all_to_all x1, blocking collectives, body(): lax.all_to_all(cot_slots, 'expert', split_axis=0, concat_axis=0, tiled=True)  37.7 us
    all_gather x1, waiting for transfers between devices, body(): lax.all_gather(got_cot.reshape(-1, width), 'dp', axis=0, tiled=True)  30.8 us
    all_to_all x1, waiting for transfers between devices, body(): lax.all_to_all(summed.astype(jnp.bfloat16).reshape(experts, slots, width)...  20.2 us
    all_to_all x1, starting transfers between devices, body(): lax.all_to_all(summed.astype(jnp.bfloat16).reshape(experts, slots, width)...  15.5 us
  transfers between devices with their start and end apart: 4, of which 3 were waited for; matrix products, arithmetic and copies ran while one was open for 7% of the time, Pallas kernels for 0%

profile of v1, /device:TPU:1, one launch (start us, length us, event | category | flops | bytes accessed | tf_op | source)
XLA Modules:
  0.0 261.8 jit_solution(5828951506605744945)
XLA Ops:
  7.2 0.0 copy-start
  7.2 0.0 copy-start.5
  7.2 0.0 copy-start.6
  7.2 0.0 copy-start.4
  7.2 0.0 all-gather.5.cloned.1.call-start
  7.3 0.8 eq.38
  8.1 0.1 fusion.24
  8.2 0.1 reduce_window_sum.11
  8.3 0.2 select_reduce_fusion
  8.4 0.1 eq.42
  8.5 0.9 fusion.5
  9.4 1.1 convolution_convert_fusion.3
  10.5 0.5 copy.24
  11.1 48.5 %all_to_all.15 = bf16[64,2,2048]{2,1,0:T(2,128)(2,1)S(1)} all-to-all(bf16[64,2,2048]{2,1,0:T(2,128)(2,1)S(1)} %copy.24), channel_id=1, replica_groups=mesh['dp'=8,'expert'=64] {'expert'}, dimensions={0} | all-to-all | bytes 1048576 | tf_op jit(solution)/shard_map/all_to_all | solution.py:67
  59.5 1.0 reshape.42
  60.5 0.0 all-gather.5.cloned.1.call-update
  60.6 0.0 all-gather.3.cloned.1.call-start
  60.6 0.0 copy-done.6
  60.6 0.0 copy-done.5
  60.6 0.2 convolution_bitcast_fusion.1
  60.9 0.0 copy-done.4
  60.9 0.4 fusion.3
  61.2 0.5 copy.22
  61.8 0.0 copy-start.3
  61.8 37.7 %all_to_all.16 = bf16[64,2,2048]{2,1,0:T(2,128)(2,1)S(1)} all-to-all(bf16[64,2,2048]{2,1,0:T(2,128)(2,1)S(1)} %copy.22), channel_id=1, replica_groups=mesh['dp'=8,'expert'=64] {'expert'}, dimensions={0} | all-to-all | bytes 1048576 | tf_op jit(solution)/shard_map/all_to_all | solution.py:68
  99.5 1.0 reshape.41
  100.5 0.0 all-gather.3.cloned.1.call-update
  100.5 0.0 reduce-scatter.2.cloned.1.call-start
  100.5 0.0 all-gather.5.cloned.1.call-done
  100.6 0.0 copy-done
  100.6 0.0 copy-start.1
  100.6 4.7 %fusion.8 = f32[1024,192]{0,1:T(8,128)} fusion(bf16[1024,2048]{1,0:T(8,128)(2,1)} %all-gather.5.cloned.1.call-done, bf16[1,192,2048]{2,1,0:T(8,128)(2,1)S(1)} %copy-done), kind=kOutput, calls=%fused_computation.17 | convolution fusion | flops 805306368 | bytes 5767168 | tf_op jit(solution)/shard_map/dot_general | solution.py:38
  105.3 0.0 copy-done.3
  105.3 0.0 copy-done.1
  105.3 0.0 copy-start.8
  105.3 2.5 fusion.11
  107.9 30.8 %all-gather.3.cloned.1.call-done = bf16[1024,2048]{1,0:T(8,128)(2,1)} async-done(((bf16[128,2048]{1,0:T(8,128)(2,1)}), bf16[1024,2048]{1,0:T(8,128)(2,1)}) %all-gather.3.cloned.1.call-update) | async-done | bytes 4194320 | tf_op jit(solution)/shard_map/all_gather | solution.py:70
  138.6 0.0 copy-done.8
  138.6 4.3 %multiply_convert_fusion.1 = (bf16[1024,192]{0,1:T(8,128)(2,1)S(1)}, bf16[1024,192]{0,1:T(8,128)(2,1)S(1)}) fusion(f32[1024,192]{0,1:T(8,128)} %fusion.8, f32[1024,192]{0,1:T(8,128)} %fusion.11, bf16[1024,2048]{1,0:T(8,128)(2,1)} %all-gather.3.cloned.1.call-done, bf16[1,192,2048]{2,1,0:T(8,128)(2,1)S(1)} %copy-done.8), kind=kOutput, calls=%fused_computation.25 | convolution fusion | flops 807862272 | bytes 7340032 | tf_op jit(solution)/shard_map/dot_general | solution.py:47
  143.0 1.3 fusion.6
  144.3 4.5 %convolution_add_fusion = f32[1024,2048]{1,0:T(8,128)} fusion(f32[1024,2048]{1,0:T(8,128)S(1)} %fusion.6, bf16[1024,192]{0,1:T(8,128)(2,1)S(1)} %get-tuple-element.4, bf16[1,192,2048]{2,1,0:T(8,128)(2,1)S(1)} %copy-done.3), kind=kOutput, calls=%fused_computation | convolution fusion | flops 807403520 | bytes 17956864 | tf_op jit(solution)/shard_map/dot_general | solution.py:58
  148.8 0.0 reduce-scatter.2.cloned.1.call-update
  148.8 59.3 %reduce-scatter.2.cloned.1.call-done = f32[128,2048]{1,0:T(8,128)} async-done(((f32[1024,2048]{1,0:T(8,128)}), f32[128,2048]{1,0:T(8,128)}) %reduce-scatter.2.cloned.1.call-update) | async-done | bytes 1048592 | tf_op jit(solution)/shard_map/reduce_scatter | solution.py:74
  208.1 1.3 convert_element_type.69
  209.4 1.1 reshape.43
  210.6 15.5 %all-to-all-start.2 = ((bf16[64,2,2048]{2,1,0:T(2,128)(2,1)}), bf16[64,2,2048]{2,1,0:T(2,128)(2,1)S(1)}, u32[]{:S(2)}, u32[]{:S(2)}) async-start(bf16[64,2,2048]{2,1,0:T(2,128)(2,1)} %reshape.43), calls=%async_computation.3 | async-start | bytes 1048576 | tf_op jit(solution)/shard_map/all_to_all | solution.py:75
  226.1 0.0 copy-start.2
  226.1 0.0 copy-start.7
  226.1 0.0 copy-start.9
  226.2 0.0 copy-start.10
  226.2 4.2 %fusion.1 = bf16[1,192,2048]{2,1,0:T(8,128)(2,1)} fusion(bf16[1024,192]{0,1:T(8,128)(2,1)S(1)} %get-tuple-element.4, bf16[1024,2048]{1,0:T(8,128)(2,1)} %all-gather.5.cloned.1.call-done), kind=kOutput, calls=%fused_computation.6 | convolution fusion | flops 805699584 | bytes 5373952 | tf_op jit(solution)/shard_map/dot_general | solution.py:56
  230.4 0.0 copy-done.2
  230.4 1.9 fusion
  232.3 0.0 copy-done.7
  232.3 0.0 copy-done.9
  232.3 0.0 copy-done.10
  232.3 1.9 fusion.2
  234.2 20.2 %all-to-all-done.2 = bf16[64,2,2048]{2,1,0:T(2,128)(2,1)S(1)} async-done(((bf16[64,2,2048]{2,1,0:T(2,128)(2,1)}), bf16[64,2,2048]{2,1,0:T(2,128)(2,1)S(1)}, u32[]{:S(2)}, u32[]{:S(2)}) %all-to-all-start.2) | async-done | bytes 524320 | tf_op jit(solution)/shard_map/all_to_all | solution.py:75
  254.4 0.9 fusion.4
  (1 shorter events, 0.0 us)
Async XLA Ops:
  7.2 93.4 %copy-start = (bf16[1,192,2048]{2,1,0:T(8,128)(2,1)S(1)}, bf16[1,192,2048]{2,1,0:T(8,128)(2,1)}, u32[]{:S(2)}) copy-start(bf16[1,192,2048]{2,1,0:T(8,128)(2,1)} %param.11) | copy-start | bytes 2359300
  7.2 53.5 %copy-start.5 = (s32[8,8]{1,0:T(8,128)S(1)}, s32[8,8]{1,0:T(8,128)}, u32[]{:S(2)}) copy-start(s32[8,8]{1,0:T(8,128)} %param.9) | copy-start | bytes 772
  7.2 53.4 %copy-start.6 = (s32[8,8]{1,0:T(8,128)S(1)}, s32[8,8]{1,0:T(8,128)}, u32[]{:S(2)}) copy-start(s32[8,8]{1,0:T(8,128)} %param.10) | copy-start | bytes 772
  7.2 53.7 %copy-start.4 = (bf16[8,2048]{1,0:T(8,128)(2,1)S(1)}, bf16[8,2048]{1,0:T(8,128)(2,1)}, u32[]{:S(2)}) copy-start(bf16[8,2048]{1,0:T(8,128)(2,1)} %param.8) | copy-start | bytes 98308
  7.2 93.3 %all-gather.5.cloned.1.call-start = ((), (), s32[]{:S(2)}) async-start(), calls=%async_computation.5 | async-start | bytes 4718592 | tf_op jit(solution)/shard_map/all_gather | solution.py:69
  60.6 78.1 %all-gather.3.cloned.1.call-start = ((), (), s32[]{:S(2)}) async-start(), calls=%async_computation.4 | async-start | bytes 4718592 | tf_op jit(solution)/shard_map/all_gather | solution.py:70
  61.8 43.6 %copy-start.3 = (bf16[1,192,2048]{2,1,0:T(8,128)(2,1)S(1)}, bf16[1,192,2048]{2,1,0:T(8,128)(2,1)}, u32[]{:S(2)}) copy-start(bf16[1,192,2048]{2,1,0:T(8,128)(2,1)} %param.12) | copy-start | bytes 2359300
  100.5 107.6 %reduce-scatter.2.cloned.1.call-start = ((), (), s32[]{:S(2)}) async-start(), calls=%async_computation.6 | async-start | bytes 9437184 | tf_op jit(solution)/shard_map/reduce_scatter | solution.py:74
  100.6 4.8 %copy-start.1 = (bf16[1024,2048]{1,0:T(8,128)(2,1)S(1)}, bf16[1024,2048]{1,0:T(8,128)(2,1)}, u32[]{:S(2)}) copy-start(bf16[1024,2048]{1,0:T(8,128)(2,1)} %all-gather.5.cloned.1.call-done) | copy-start | bytes 12582916
  105.3 33.3 %copy-start.8 = (bf16[1,192,2048]{2,1,0:T(8,128)(2,1)S(1)}, bf16[1,192,2048]{2,1,0:T(8,128)(2,1)}, u32[]{:S(2)}) copy-start(bf16[1,192,2048]{2,1,0:T(8,128)(2,1)} %param.13) | copy-start | bytes 2359300
  210.6 43.8 %all-to-all-start.2 = ((bf16[64,2,2048]{2,1,0:T(2,128)(2,1)}), bf16[64,2,2048]{2,1,0:T(2,128)(2,1)S(1)}, u32[]{:S(2)}, u32[]{:S(2)}) async-start(bf16[64,2,2048]{2,1,0:T(2,128)(2,1)} %reshape.43), calls=%async_computation.3 | async-start | bytes 1048576 | tf_op jit(solution)/shard_map/all_to_all | solution.py:75
  226.1 4.3 %copy-start.2 = (bf16[1024,2048]{1,0:T(8,128)(2,1)S(1)}, bf16[1024,2048]{1,0:T(8,128)(2,1)}, u32[]{:S(2)}) copy-start(bf16[1024,2048]{1,0:T(8,128)(2,1)} %all-gather.5.cloned.1.call-done) | copy-start | bytes 12582916
  226.1 6.2 %copy-start.7 = (bf16[1024,2048]{1,0:T(8,128)(2,1)S(1)}, bf16[1024,2048]{1,0:T(8,128)(2,1)}, u32[]{:S(2)}) copy-start(bf16[1024,2048]{1,0:T(8,128)(2,1)} %all-gather.3.cloned.1.call-done) | copy-start | bytes 12582916
  226.1 6.2 %copy-start.9 = (f32[1024,192]{0,1:T(8,128)S(1)}, f32[1024,192]{0,1:T(8,128)}, u32[]{:S(2)}) copy-start(f32[1024,192]{0,1:T(8,128)} %fusion.8) | copy-start | bytes 2359300
  226.2 6.1 %copy-start.10 = (f32[1024,192]{0,1:T(8,128)S(1)}, f32[1024,192]{0,1:T(8,128)}, u32[]{:S(2)}) copy-start(f32[1024,192]{0,1:T(8,128)} %fusion.11) | copy-start | bytes 2359300
Sparse Core Ops, SparseCore 0:
  60.7 35.3 all-gather.4
  100.6 37.9 all-gather.2
  148.9 59.1 reduce-scatter.1

commit v2 on v1

v2 whole, which is shorter than its diff:
```python
import functools

import jax
import jax.numpy as jnp
from jax import lax
from jax.experimental import pallas as pl
from jax.experimental.pallas import tpu as pltpu
from jax.sharding import PartitionSpec as P

MESH = pl.DeviceIdType.MESH
f32 = jnp.float32
bf16 = jnp.bfloat16

D = 2048
H = 192
NX, NY, NZ = 4, 4, 16
META = 128
HALF = D // 2
PIECE = 16
PLANE = NY * PIECE
COPIES = 192

OFFSETS = (0, -1, 1, -2, 2, -3, 3, -4, 4, -5, 5, -6, 6, -7, 7, -8)
POS = {offset: place for place, offset in enumerate(OFFSETS)}


def dot_nt(a, b):
    return lax.dot_general(a, b, (((1,), (1,)), ((), ())), preferred_element_type=f32)


def dot(a, b):
    return jnp.dot(a, b, preferred_element_type=f32)


def kernel(
    tok_ref, cot_ref, ids_ref, codes_ref, wg_ref, wu_ref, wd_ref,
    tg_ref, gg_ref, gu_ref, gd_ref,
    gz, sel, unsel, xc, h_t, dg_t, du_t, p_own, p_sib, p_got,
    xs_o, xs_l, xs_r, xr_o, xr_l, xr_r, ys, yr, zp, zs_m, zs_p, zr_m, zr_p,
    send_sem, recv_sem,
):
    me_dp = lax.axis_index("dp")
    me_e = lax.axis_index("expert")
    x, core = me_dp // 2, me_dp % 2
    y, z = me_e // NZ, me_e % NZ

    def at(dx=0, dy=0, dz=0, flip=False):
        other = (1 - core) if flip else core
        return (
            ((x + dx + NX) % NX) * 2 + other,
            ((y + dy + NY) % NY) * NZ + (z + dz + NZ) % NZ,
        )

    x_up, x_dn = at(dx=1), at(dx=-1)
    z_up, z_dn = at(dz=1), at(dz=-1)
    sibling = at(flip=True)
    y_peer = {1: at(dy=1), 2: at(dy=-1), 3: at(dy=2)}
    y_back = {1: at(dy=-1), 2: at(dy=1), 3: at(dy=2)}

    counter = [0]
    started = []

    def copy(src, dst, device):
        number = counter[0]
        counter[0] += 1
        made = pltpu.make_async_remote_copy(
            src_ref=src, dst_ref=dst, send_sem=send_sem.at[number],
            recv_sem=recv_sem.at[number], device_id=device, device_id_type=MESH,
        )
        started.append(made)
        made.start()
        return made

    barrier = pltpu.get_barrier_semaphore()
    partners = (z_up, z_dn, at(dy=1), at(dy=-1), at(dy=2), x_up, x_dn, sibling)
    for partner in partners:
        pl.semaphore_signal(barrier, inc=1, device_id=partner, device_id_type=MESH)

    rows = jnp.concatenate([tok_ref[...].astype(f32), cot_ref[...].astype(f32)], axis=0)
    gz[0, :, 0:D] = rows.astype(bf16)
    codes = codes_ref[...]
    parts = (ids_ref[...], codes // 8, codes % 8)
    spread_row = lax.broadcasted_iota(jnp.int32, (8, META), 0)
    spread_col = lax.broadcasted_iota(jnp.int32, (8, META), 1)
    meta = jnp.zeros((8, META), f32)
    for number, part in enumerate(parts):
        spread = (spread_col == spread_row + 8 * number).astype(f32)
        meta = meta + dot(part.astype(f32).astype(bf16), spread.astype(bf16))
    gz[0, :, D:D + META] = jnp.concatenate([meta, meta], axis=0).astype(bf16)

    pl.semaphore_wait(barrier, len(partners))

    cuts = ((0, HALF), (HALF, D + META - HALF))

    def z_send(place, to_place, device):
        return [
            copy(
                gz.at[place, :, pl.ds(first, size)],
                gz.at[to_place, :, pl.ds(first, size)],
                device,
            )
            for first, size in cuts
        ]

    up = z_send(POS[0], POS[-1], z_up)
    down = z_send(POS[0], POS[1], z_dn)

    def z_step(k, up, down):
        next_up, next_down = [], []
        for cut, (first, size) in enumerate(cuts):
            up[cut].wait_recv()
            if k < 8:
                next_up.append(copy(
                    gz.at[POS[-k], :, pl.ds(first, size)],
                    gz.at[POS[-k - 1], :, pl.ds(first, size)], z_up))
            if k <= 7:
                down[cut].wait_recv()
            if k < 7:
                next_down.append(copy(
                    gz.at[POS[k], :, pl.ds(first, size)],
                    gz.at[POS[k + 1], :, pl.ds(first, size)], z_dn))
        return next_up, next_down

    lane = lax.broadcasted_iota(jnp.int32, (128, 128), 1)
    row = lax.broadcasted_iota(jnp.int32, (128, 128), 0)
    lane_kind, lane_dy, lane_slot = lane // 64, (lane % 64) // 16, lane % 16
    step_y = jnp.where(lane_dy == 1, 1, jnp.where(lane_dy == 2, NY - 1, jnp.where(lane_dy == 3, 2, 0)))
    lane_expert = (((y + step_y) % NY) * NZ + z).astype(f32)
    fits = (lane_kind == (row % 16) // 8) & (row // 16 == lane_slot // 2)
    earlier = ((row // 8 == lane // 8) & (lane < row)).astype(f32).astype(bf16)
    lane_rank = (lane_slot % 2).astype(f32)

    def base(c, q):
        return (c * 8 + q) * PLANE

    def select(c):
        block = gz[8 * c:8 * c + 8]
        table = block[:, :, D:D + META].reshape(128, META).astype(f32)
        hit = jnp.zeros((128, 128), f32)
        high = jnp.zeros((128, 128), f32)
        low = jnp.zeros((128, 128), f32)
        for i in range(8):
            same = table[:, i:i + 1] == lane_expert
            hit = hit + jnp.where(same, 1.0, 0.0)
            high = high + jnp.where(same, table[:, 8 + i:9 + i], 0.0)
            low = low + jnp.where(same, table[:, 16 + i:17 + i], 0.0)
        rank = dot(earlier, hit.astype(bf16))
        mine = jnp.where(fits & (rank == lane_rank), hit, 0.0)
        unsel[c] = mine.astype(bf16)
        is_cot = lane_kind == 1
        first = (mine * jnp.where(is_cot, high * (1.0 / 128.0), 1.0)).T.astype(bf16)
        second = (mine * jnp.where(is_cot, low * (1.0 / 1024.0), 0.0)).T.astype(bf16)
        for j in range(4):
            cols = pl.ds(512 * j, 512)
            data = gz[8 * c:8 * c + 8, :, cols].reshape(128, 512)
            got = (dot(first, data) + dot(second, data)).astype(bf16)
            for kind in range(2):
                to = pl.ds(kind * D + 512 * j, 512)
                xc[pl.ds(base(c, 0), PIECE), to] = got[64 * kind:64 * kind + 16]
                sel[c, :, :, to] = got[64 * kind + 16:64 * kind + 64].reshape(3, 16, 512)

    def y_send(c):
        return {
            p: copy(sel.at[c, p - 1], xc.at[pl.ds(base(c, 0) + p * PIECE, PIECE), :], y_peer[p])
            for p in (1, 2, 3)
        }

    def piece(c, q, p):
        return xc.at[pl.ds(base(c, q) + p * PIECE, PIECE), :]

    def half_piece(c, q, p, kind):
        return xc.at[pl.ds(base(c, q) + p * PIECE, PIECE), pl.ds(kind * D, D)]

    from_dn, from_up, far_in, far_cot, sib = {}, {}, {}, {}, {}

    def x_first(c, p):
        from_dn[c, p] = copy(piece(c, 0, p), piece(c, 1, p), x_up)
        from_up[c, p] = copy(piece(c, 0, p), piece(c, 2, p), x_dn)
        sib[c, 0, p] = copy(piece(c, 0, p), piece(c, 4, p), sibling)

    def x_forward(c, p):
        from_dn[c, p].wait_recv()
        far_in[c, p] = copy(half_piece(c, 1, p, 0), half_piece(c, 3, p, 0), x_up)
        sib[c, 1, p] = copy(piece(c, 1, p), piece(c, 5, p), sibling)
        from_up[c, p].wait_recv()
        far_cot[c, p] = copy(half_piece(c, 2, p, 1), half_piece(c, 3, p, 1), x_dn)
        sib[c, 2, p] = copy(piece(c, 2, p), piece(c, 6, p), sibling)

    def x_last(c, p):
        far_in[c, p].wait_recv()
        far_cot[c, p].wait_recv()
        sib[c, 3, p] = copy(piece(c, 3, p), piece(c, 7, p), sibling)

    def forward(c, half):
        if half == 1:
            for q in range(4):
                for p in range(4):
                    sib[c, q, p].wait_recv()
        first = base(c, 4 * half)
        rows_here = pl.ds(first, 256)
        pre_gate = dot_nt(xc[rows_here, 0:D], wg_ref[0])
        pre_up = dot_nt(xc[rows_here, 0:D], wu_ref[0])
        d_hidden = dot_nt(xc[rows_here, D:2 * D], wd_ref[0])
        sig = jax.nn.sigmoid(pre_gate)
        active = pre_gate * sig
        hidden = active * pre_up
        d_up = d_hidden * active
        d_gate = d_hidden * pre_up * sig * (1.0 + pre_gate * (1.0 - sig))
        h_t[:, rows_here] = hidden.T.astype(bf16)
        du_t[:, rows_here] = d_up.T.astype(bf16)
        dg_t[:, rows_here] = d_gate.T.astype(bf16)
        d_up, d_gate = d_up.astype(bf16), d_gate.astype(bf16)
        into = p_sib if half else p_own
        for j in range(4):
            cols = pl.ds(512 * j, 512)
            part = dot(d_gate, wg_ref[0, :, cols]) + dot(d_up, wu_ref[0, :, cols])
            into[c, :, cols] = part.astype(bf16)

    def core_send(c):
        return {
            q: copy(p_sib.at[c, pl.ds(q * PLANE, PLANE)], p_got.at[c, pl.ds(q * PLANE, PLANE)], sibling)
            for q in (3, 2, 1, 0)
        }

    def pair(c, q, cols):
        here = pl.ds(q * PLANE, PLANE)
        return p_own[c, here, cols].astype(f32) + p_got[c, here, cols].astype(f32)

    left, right, both = pl.ds(0, HALF), pl.ds(HALF, HALF), pl.ds(0, D)

    def x_return_first(c, core_copies):
        core_copies[3].wait_recv()
        xs_o[c] = pair(c, 3, both).astype(bf16)
        relay_r = copy(xs_o.at[c, :, left], xr_o.at[c, :, left], x_up)
        relay_l = copy(xs_o.at[c, :, right], xr_o.at[c, :, right], x_dn)
        core_copies[2].wait_recv()
        xs_r[c, :, right] = pair(c, 2, right).astype(bf16)
        r_plain = copy(xs_r.at[c, :, right], xr_l.at[c, :, right], x_up)
        core_copies[1].wait_recv()
        xs_l[c, :, left] = pair(c, 1, left).astype(bf16)
        l_plain = copy(xs_l.at[c, :, left], xr_r.at[c, :, left], x_dn)
        return relay_r, relay_l, r_plain, l_plain

    def x_return_second(c, relay_r, relay_l, r_plain, l_plain):
        relay_r.wait_recv()
        xs_r[c, :, left] = (pair(c, 2, left) + xr_o[c, :, left].astype(f32)).astype(bf16)
        r_sum = copy(xs_r.at[c, :, left], xr_l.at[c, :, left], x_up)
        relay_l.wait_recv()
        xs_l[c, :, right] = (pair(c, 1, right) + xr_o[c, :, right].astype(f32)).astype(bf16)
        l_sum = copy(xs_l.at[c, :, right], xr_r.at[c, :, right], x_dn)
        return r_plain, l_plain, r_sum, l_sum

    def y_return(c, core_copies, arriving):
        core_copies[0].wait_recv()
        for one in arriving:
            one.wait_recv()
        sends = {}
        for side, cols in enumerate((left, right)):
            total = pair(c, 0, cols) + xr_l[c, :, cols].astype(f32) + xr_r[c, :, cols].astype(f32)
            total = total.astype(bf16)
            yr[c, side, 0] = total[0:PIECE]
            ys[c, side] = total[PIECE:].reshape(3, PIECE, HALF)
        for p in (3, 1, 2):
            sends[p] = copy(ys.at[c, :, p - 1], yr.at[c, :, p], y_back[p])
        return sends

    def unselect(c, y_copies):
        for p in (1, 2, 3):
            y_copies[p].wait_recv()
        part = dot(unsel[c], yr[c].reshape(128, HALF))
        zp[8 * c:8 * c + 8] = part.reshape(8, 16, HALF)

    def grad_tile(kind, j):
        out, lhs, shift = ((gg_ref, dg_t, 0), (gu_ref, du_t, 0), (gd_ref, h_t, D))[kind]
        data = xc[:, pl.ds(shift + 512 * j, 512)]
        out[0, :, pl.ds(512 * j, 512)] = dot(lhs[...], data).astype(bf16)

    tiles = [(kind, j) for kind in range(3) for j in range(4)]

    def some_grads(count):
        for _ in range(min(count, len(tiles))):
            grad_tile(*tiles.pop(0))

    for k in range(1, 5):
        up, down = z_step(k, up, down)
    select(0)
    y0 = y_send(0)
    x_first(0, 0)
    up, down = z_step(5, up, down)
    y0[1].wait_recv()
    x_first(0, 1)
    y0[2].wait_recv()
    x_first(0, 2)
    up, down = z_step(6, up, down)
    y0[3].wait_recv()
    x_first(0, 3)
    x_forward(0, 0)
    up, down = z_step(7, up, down)
    x_forward(0, 1)
    up, down = z_step(8, up, down)
    select(1)
    y1 = y_send(1)
    x_first(1, 0)
    x_last(0, 0)
    x_forward(0, 2)
    y1[1].wait_recv()
    x_first(1, 1)
    y1[2].wait_recv()
    x_first(1, 2)
    y1[3].wait_recv()
    x_first(1, 3)
    x_last(0, 1)
    x_forward(0, 3)
    x_last(0, 2)
    x_forward(1, 0)
    x_last(0, 3)
    forward(0, 0)
    x_forward(1, 1)
    forward(0, 1)
    x_forward(1, 2)
    core0 = core_send(0)
    x_last(1, 0)
    x_forward(1, 3)
    x_last(1, 1)
    x0 = x_return_first(0, core0)
    x_last(1, 2)
    x_last(1, 3)
    forward(1, 0)
    x0 = x_return_second(0, *x0)
    forward(1, 1)
    core1 = core_send(1)
    back0 = y_return(0, core0, x0)
    x1 = x_return_first(1, core1)
    some_grads(2)
    x1 = x_return_second(1, *x1)
    unselect(0, back0)
    some_grads(2)
    back1 = y_return(1, core1, x1)
    some_grads(2)
    unselect(1, back1)

    got_m, got_p = None, None
    for j in range(8):
        block = zp[POS[-(8 - j)]]
        if got_m is not None:
            got_m.wait_recv()
            block = block + zr_m[j - 1]
        zs_m[j] = block
        got_m = copy(zs_m.at[j], zr_m.at[j], z_dn)
        if j < 7:
            block = zp[POS[7 - j]]
            if got_p is not None:
                got_p.wait_recv()
                block = block + zr_p[j - 1]
            zs_p[j] = block
            got_p = copy(zs_p.at[j], zr_p.at[j], z_up)
        some_grads(1)
    some_grads(len(tiles))
    got_p.wait_recv()
    got_m.wait_recv()
    total = zp[0] + zr_m[7] + zr_p[6]
    tg_ref[:, 0:HALF] = total[0:8].astype(bf16)
    tg_ref[:, HALF:D] = total[8:16].astype(bf16)

    for made in started:
        made.wait_send()


def body(tokens, cotangent, expert_ids, gate_codes, w_gate, w_up, w_down):
    vmem = pl.BlockSpec(memory_space=pltpu.VMEM)
    return pl.pallas_call(
        kernel,
        out_shape=(
            jax.ShapeDtypeStruct((8, D), bf16),
            jax.ShapeDtypeStruct((1, H, D), bf16),
            jax.ShapeDtypeStruct((1, H, D), bf16),
            jax.ShapeDtypeStruct((1, H, D), bf16),
        ),
        in_specs=[vmem] * 7,
        out_specs=(vmem,) * 4,
        scratch_shapes=[
            pltpu.VMEM((NZ, 16, D + META), bf16),
            pltpu.VMEM((2, 3, PIECE, 2 * D), bf16),
            pltpu.VMEM((2, 128, 128), bf16),
            pltpu.VMEM((1024, 2 * D), bf16),
            pltpu.VMEM((H, 1024), bf16),
            pltpu.VMEM((H, 1024), bf16),
            pltpu.VMEM((H, 1024), bf16),
            pltpu.VMEM((2, 256, D), bf16),
            pltpu.VMEM((2, 256, D), bf16),
            pltpu.VMEM((2, 256, D), bf16),
        ]
        + [pltpu.VMEM((2, PLANE, D), bf16)] * 6
        + [
            pltpu.VMEM((2, 2, 3, PIECE, HALF), bf16),
            pltpu.VMEM((2, 2, 4, PIECE, HALF), bf16),
            pltpu.VMEM((NZ, 16, HALF), f32),
            pltpu.VMEM((8, 16, HALF), f32),
            pltpu.VMEM((7, 16, HALF), f32),
            pltpu.VMEM((8, 16, HALF), f32),
            pltpu.VMEM((7, 16, HALF), f32),
            pltpu.SemaphoreType.DMA((COPIES,)),
            pltpu.SemaphoreType.DMA((COPIES,)),
        ],
        compiler_params=pltpu.CompilerParams(
            collective_id=0, has_side_effects=True, vmem_limit_bytes=52 * 1024 * 1024
        ),
        name="expert_layer_backward",
    )(tokens, cotangent, expert_ids, gate_codes, w_gate, w_up, w_down)


def solution(mesh):
    placed = (
        P(("dp", "expert"), None),
        P(("dp", "expert"), None),
        P(("dp", "expert"), None),
        P(("dp", "expert"), None),
        P("expert", "dp", None),
        P("expert", "dp", None),
        P("expert", "dp", None),
    )
    return jax.shard_map(
        body,
        mesh=mesh,
        in_specs=placed,
        out_specs=(
            P(("dp", "expert"), None),
            P("expert", "dp", None),
            P("expert", "dp", None),
            P("expert", "dp", None),
        ),
        check_vma=False,
    )
```

time: 265 us -> 132 us (0.50)
  the two profiles are of different devices: /device:TPU:1 before, /device:TPU:8 now
where the time goes in v2:
time: 132 us
  Pallas kernels  124 us (94%)
  local copies, waits for them, and re-layouts  6.67 us (5%)
    pallas_call x1, Pallas kernels, body(): pl.pallas_call(kernel, out_shape=(jax.ShapeDtypeStruct((8, D), bf16), jax...  124 us
    unnamed x14, local copies, waits for them, and re-layouts  6.67 us

profile of v2, /device:TPU:8, one launch (start us, length us, event | category | flops | bytes accessed | tf_op | source)
XLA Modules:
  0.0 131.6 jit_solution(3882162633851069380)
XLA Ops:
  0.6 0.0 copy-start
  0.6 0.7 copy-done
  1.4 0.0 copy-start.1
  1.4 0.8 copy-done.1
  2.2 0.0 copy-start.2
  2.2 0.7 copy-done.2
  2.8 0.0 copy-start.3
  2.8 0.7 copy-done.3
  3.5 124.2 %expert_layer_backward.1 = (bf16[8,2048]{1,0:T(8,128)(2,1)S(1)}, bf16[1,192,2048]{2,1,0:T(8,128)(2,1)S(1)}, bf16[1,192,2048]{2,1,0:T(8,128)(2,1)S(1)}, bf16[1,192,2048]{2,1,0:T(8,128)(2,1)}) custom-call(bf16[8,2048]{1,0:T(8,128)(2,1)S(1)} %copy-done, bf16[8,2048]{1,0:T(8,128)(2,1)S(1)} %copy-done.1, s32[8,8]{1,0:T(8,128)S(1)} %copy-done.2, ...), custom_call_target="tpu_custom_call" | custom-call | tf_op jit(solution)/shard_map/expert_layer_backward/pallas_call | solution.py:371
  127.8 0.6 copy.15
  128.4 0.9 copy.16
  129.3 0.0 copy-start.4
  129.3 0.9 copy.17
  130.2 0.5 copy-done.4
  130.7 0.9 copy.18
Async XLA Ops:
  0.6 0.8 copy-start
  1.4 0.8 copy-start.1
  2.2 0.7 copy-start.2
  2.8 0.7 copy-start.3
  129.3 1.4 %copy-start.4 = (bf16[1,192,2048]{2,1,0:T(8,128)(2,1)S(1)}, bf16[1,192,2048]{2,1,0:T(8,128)(2,1)}, u32[]{:S(2)}) copy-start(bf16[1,192,2048]{2,1,0:T(8,128)(2,1)} %get-tuple-element.11) | copy-start | bytes 2359300

commit v3 on v2

v3 whole, which is shorter than its diff:
```python
import functools

import jax
import jax.numpy as jnp
from jax import lax
from jax.experimental import pallas as pl
from jax.experimental.pallas import tpu as pltpu
from jax.sharding import PartitionSpec as P

MESH = pl.DeviceIdType.MESH
f32 = jnp.float32
bf16 = jnp.bfloat16

D = 2048
H = 192
NX, NY, NZ = 4, 4, 16
META = 128
HALF = D // 2
PIECE = 16
PLANE = NY * PIECE
COPIES = 192

OFFSETS = (0, -1, 1, -2, 2, -3, 3, -4, 4, -5, 5, -6, 6, -7, 7, -8)
POS = {offset: place for place, offset in enumerate(OFFSETS)}


def dot_nt(a, b):
    return lax.dot_general(a, b, (((1,), (1,)), ((), ())), preferred_element_type=f32)


def dot(a, b):
    return jnp.dot(a, b, preferred_element_type=f32)


def kernel(
    tok_hbm, cot_hbm, ids_hbm, codes_hbm, wg_hbm, wu_hbm, wd_hbm,
    tg_hbm, gg_hbm, gu_hbm, gd_hbm,
    tok_ref, cot_ref, ids_ref, codes_ref, wg_ref, wu_ref, wd_ref, gz, gz_far, sel, unsel, xc, h_t, dg_t, du_t, p_own, p_sib, p_got,
    xs_o, xs_l, xs_r, xr_o, xr_l, xr_r, ys, yr, zp, zs, zr_m1, zr_m2, zr_p1, zr_p2,
    tg_ref, gg_ref, gu_ref, gd_ref,
    send_sem, recv_sem, load_sem, store_sem,
):
    me_dp = lax.axis_index("dp")
    me_e = lax.axis_index("expert")
    x, core = me_dp // 2, me_dp % 2
    y, z = me_e // NZ, me_e % NZ

    def at(dx=0, dy=0, dz=0, flip=False):
        other = (1 - core) if flip else core
        return (
            ((x + dx + NX) % NX) * 2 + other,
            ((y + dy + NY) % NY) * NZ + (z + dz + NZ) % NZ,
        )

    x_up, x_dn, x_far = at(dx=1), at(dx=-1), at(dx=2)
    z_up, z_dn, z_up2, z_dn2 = at(dz=1), at(dz=-1), at(dz=2), at(dz=-2)
    sibling = at(flip=True)
    y_peer = {1: at(dy=1), 2: at(dy=-1), 3: at(dy=2)}
    y_back = {1: at(dy=-1), 2: at(dy=1), 3: at(dy=2)}

    counter = [0]
    started = []

    def copy(src, dst, device):
        number = counter[0]
        counter[0] += 1
        made = pltpu.make_async_remote_copy(
            src_ref=src, dst_ref=dst, send_sem=send_sem.at[number],
            recv_sem=recv_sem.at[number], device_id=device, device_id_type=MESH,
        )
        started.append(made)
        made.start()
        return made

    barrier = pltpu.get_barrier_semaphore()
    partners = (z_up, z_dn, z_up2, z_dn2, at(dy=1), at(dy=-1), at(dy=2), x_up, x_dn, x_far, sibling)
    for partner in partners:
        pl.semaphore_signal(barrier, inc=1, device_id=partner, device_id_type=MESH)

    loads = [
        pltpu.make_async_copy(src, dst, load_sem.at[number])
        for number, (src, dst) in enumerate(
            ((tok_hbm, tok_ref), (cot_hbm, cot_ref), (ids_hbm, ids_ref), (codes_hbm, codes_ref),
             (wg_hbm.at[0], wg_ref), (wu_hbm.at[0], wu_ref), (wd_hbm.at[0], wd_ref))
        )
    ]
    for load in loads:
        load.start()
    for load in loads[0:4]:
        load.wait()
    rows = jnp.concatenate([tok_ref[...].astype(f32), cot_ref[...].astype(f32)], axis=0)
    gz[0, :, 0:D] = rows.astype(bf16)
    codes = codes_ref[...]
    spread_row = lax.broadcasted_iota(jnp.int32, (8, META), 0)
    spread_col = lax.broadcasted_iota(jnp.int32, (8, META), 1)
    meta = jnp.zeros((8, META), f32)
    for number, part in enumerate((ids_ref[...], codes // 8, codes % 8)):
        spread = (spread_col == spread_row + 8 * number).astype(f32)
        meta = meta + dot(part.astype(f32).astype(bf16), spread.astype(bf16))
    gz[0, :, D:D + META] = jnp.concatenate([meta, meta], axis=0).astype(bf16)
    pl.semaphore_wait(barrier, len(partners))

    cuts = ((0, HALF), (HALF, D + META - HALF))
    ring_got = {}

    def ring_send(plane, place, to_place, cut, device):
        cols = pl.ds(*cuts[cut])
        held = (gz, gz_far)[plane]
        ring_got[plane, to_place, cut] = copy(
            held.at[POS[place], :, cols], held.at[POS[to_place], :, cols], device
        )

    def ring(plane, k):
        for cut in range(2):
            for way, last, device in ((-1, 8, z_up), (1, 7, z_dn)):
                if k and k <= last:
                    ring_got[plane, way * k, cut].wait_recv()
                if k < last:
                    ring_send(plane, way * k, way * (k + 1), cut, device)

    lane = lax.broadcasted_iota(jnp.int32, (128, 128), 1)
    row = lax.broadcasted_iota(jnp.int32, (128, 128), 0)
    lane_kind, lane_dy, lane_slot = lane // 64, (lane % 64) // 16, lane % 16
    step_y = jnp.where(lane_dy == 1, 1, jnp.where(lane_dy == 2, NY - 1, jnp.where(lane_dy == 3, 2, 0)))
    lane_expert = (((y + step_y) % NY) * NZ + z).astype(f32)
    fits = (lane_kind == (row % 16) // 8) & (row // 16 == lane_slot // 2)
    earlier = ((row // 8 == lane // 8) & (lane < row)).astype(f32).astype(bf16)
    lane_rank = (lane_slot % 2).astype(f32)

    def base(c, q):
        return (c * 8 + q) * PLANE

    def select(c, plane):
        blocks = (gz, gz_far)[plane]
        to_row = base(c, 3 * plane)
        table = blocks[8 * c:8 * c + 8, :, D:D + META].reshape(128, META).astype(f32)
        hit = jnp.zeros((128, 128), f32)
        high = jnp.zeros((128, 128), f32)
        low = jnp.zeros((128, 128), f32)
        for i in range(8):
            same = table[:, i:i + 1] == lane_expert
            hit = hit + jnp.where(same, 1.0, 0.0)
            high = high + jnp.where(same, table[:, 8 + i:9 + i], 0.0)
            low = low + jnp.where(same, table[:, 16 + i:17 + i], 0.0)
        rank = dot(earlier, hit.astype(bf16))
        mine = jnp.where(fits & (rank == lane_rank), hit, 0.0)
        if plane == 0:
            unsel[c] = mine.astype(bf16)
        is_cot = lane_kind == 1
        first = (mine * jnp.where(is_cot, high * (1.0 / 128.0), 1.0)).T.astype(bf16)
        second = (mine * jnp.where(is_cot, low * (1.0 / 1024.0), 0.0)).T.astype(bf16)
        for j in range(4):
            cols = pl.ds(512 * j, 512)
            data = blocks[8 * c:8 * c + 8, :, cols].reshape(128, 512)
            got = (dot(first, data) + dot(second, data)).astype(bf16)
            for kind in range(2):
                to = pl.ds(kind * D + 512 * j, 512)
                xc[pl.ds(to_row, PIECE), to] = got[64 * kind:64 * kind + 16]
                sel[plane, c, :, :, to] = got[64 * kind + 16:64 * kind + 64].reshape(3, 16, 512)

    def y_send(c, plane):
        row = base(c, 3 * plane)
        return {
            p: copy(sel.at[plane, c, p - 1], xc.at[pl.ds(row + p * PIECE, PIECE), :], y_peer[p])
            for p in (1, 2, 3)
        }

    def piece(c, q, p):
        return xc.at[pl.ds(base(c, q) + p * PIECE, PIECE), :]

    from_dn, from_up, sib = {}, {}, {}

    def x_first(c, p):
        from_dn[c, p] = copy(piece(c, 0, p), piece(c, 1, p), x_up)
        from_up[c, p] = copy(piece(c, 0, p), piece(c, 2, p), x_dn)
        to_sibling(c, 0, p)

    def to_sibling(c, q, p):
        sib[c, q, p] = copy(piece(c, q, p), piece(c, q + 4, p), sibling)

    def x_got(c, p):
        from_dn[c, p].wait_recv()
        to_sibling(c, 1, p)
        from_up[c, p].wait_recv()
        to_sibling(c, 2, p)

    def far_y_got(c, copies):
        to_sibling(c, 3, 0)
        for p in (1, 2, 3):
            copies[p].wait_recv()
            to_sibling(c, 3, p)

    def forward(c, half):
        if half == 1:
            for q in range(4):
                for p in range(4):
                    sib[c, q, p].wait_recv()
        first = base(c, 4 * half)
        rows_here = pl.ds(first, 256)
        pre_gate = dot_nt(xc[rows_here, 0:D], wg_ref[...])
        pre_up = dot_nt(xc[rows_here, 0:D], wu_ref[...])
        d_hidden = dot_nt(xc[rows_here, D:2 * D], wd_ref[...])
        sig = jax.nn.sigmoid(pre_gate)
        active = pre_gate * sig
        hidden = active * pre_up
        d_up = d_hidden * active
        d_gate = d_hidden * pre_up * sig * (1.0 + pre_gate * (1.0 - sig))
        h_t[:, rows_here] = hidden.T.astype(bf16)
        du_t[:, rows_here] = d_up.T.astype(bf16)
        dg_t[:, rows_here] = d_gate.T.astype(bf16)
        d_up, d_gate = d_up.astype(bf16), d_gate.astype(bf16)
        into = p_sib if half else p_own
        for j in range(4):
            cols = pl.ds(512 * j, 512)
            part = dot(d_gate, wg_ref[:, cols]) + dot(d_up, wu_ref[:, cols])
            into[c, :, cols] = part.astype(bf16)

    def core_send(c):
        return {
            q: copy(p_sib.at[c, pl.ds(q * PLANE, PLANE)], p_got.at[c, pl.ds(q * PLANE, PLANE)], sibling)
            for q in (3, 2, 1, 0)
        }

    def pair(c, q, cols):
        here = pl.ds(q * PLANE, PLANE)
        return p_own[c, here, cols].astype(f32) + p_got[c, here, cols].astype(f32)

    left, right, both = pl.ds(0, HALF), pl.ds(HALF, HALF), pl.ds(0, D)

    def x_return_first(c, core_copies):
        core_copies[3].wait_recv()
        xs_o[c] = pair(c, 3, both).astype(bf16)
        relay_r = copy(xs_o.at[c, :, left], xr_o.at[c, :, left], x_up)
        relay_l = copy(xs_o.at[c, :, right], xr_o.at[c, :, right], x_dn)
        core_copies[2].wait_recv()
        xs_r[c, :, right] = pair(c, 2, right).astype(bf16)
        r_plain = copy(xs_r.at[c, :, right], xr_l.at[c, :, right], x_up)
        core_copies[1].wait_recv()
        xs_l[c, :, left] = pair(c, 1, left).astype(bf16)
        l_plain = copy(xs_l.at[c, :, left], xr_r.at[c, :, left], x_dn)
        return relay_r, relay_l, r_plain, l_plain

    def x_return_second(c, relay_r, relay_l, r_plain, l_plain):
        relay_r.wait_recv()
        xs_r[c, :, left] = (pair(c, 2, left) + xr_o[c, :, left].astype(f32)).astype(bf16)
        r_sum = copy(xs_r.at[c, :, left], xr_l.at[c, :, left], x_up)
        relay_l.wait_recv()
        xs_l[c, :, right] = (pair(c, 1, right) + xr_o[c, :, right].astype(f32)).astype(bf16)
        l_sum = copy(xs_l.at[c, :, right], xr_r.at[c, :, right], x_dn)
        return r_plain, l_plain, r_sum, l_sum

    def y_return(c, core_copies, arriving):
        core_copies[0].wait_recv()
        for one in arriving:
            one.wait_recv()
        sends = {}
        for side, cols in enumerate((left, right)):
            total = pair(c, 0, cols) + xr_l[c, :, cols].astype(f32) + xr_r[c, :, cols].astype(f32)
            total = total.astype(bf16)
            yr[c, side, 0] = total[0:PIECE]
            ys[c, side] = total[PIECE:].reshape(3, PIECE, HALF)
        for p in (3, 1, 2):
            sends[p] = copy(ys.at[c, :, p - 1], yr.at[c, :, p], y_back[p])
        return sends

    def unselect(c, y_copies):
        for p in (1, 2, 3):
            y_copies[p].wait_recv()
        part = dot(unsel[c], yr[c].reshape(128, HALF))
        zp[8 * c:8 * c + 8] = part.reshape(8, 16, HALF)

    stores = []

    def store(src, dst):
        stores.append(pltpu.make_async_copy(src, dst, store_sem.at[len(stores)]))
        stores[-1].start()

    def grad_tile(kind, j):
        out, lhs, shift = ((gg_ref, dg_t, 0), (gu_ref, du_t, 0), (gd_ref, h_t, D))[kind]
        data = xc[:, pl.ds(shift + 512 * j, 512)]
        out[:, pl.ds(512 * j, 512)] = dot(lhs[...], data).astype(bf16)
        if j == 3:
            store(out, (gg_hbm, gu_hbm, gd_hbm)[kind].at[0])

    tiles = [(kind, j) for kind in range(3) for j in range(4)]

    def some_grads(count):
        for _ in range(min(count, len(tiles))):
            grad_tile(*tiles.pop(0))

    ring(0, 0)
    raw = copy(gz.at[0], gz_far.at[0], x_far)
    ring(0, 1)
    raw.wait_recv()
    ring(1, 0)
    ring(0, 2)
    ring(1, 1)
    ring(0, 3)
    ring(1, 2)
    ring(0, 4)
    select(0, 0)
    y0 = y_send(0, 0)
    x_first(0, 0)
    ring(1, 3)
    ring(0, 5)
    ring(1, 4)
    select(0, 1)
    far_y0 = y_send(0, 1)
    ring(0, 6)
    y0[1].wait_recv()
    x_first(0, 1)
    y0[2].wait_recv()
    x_first(0, 2)
    ring(1, 5)
    y0[3].wait_recv()
    x_first(0, 3)
    ring(0, 7)
    ring(1, 6)
    x_got(0, 0)
    ring(0, 8)
    select(1, 0)
    y1 = y_send(1, 0)
    x_first(1, 0)
    ring(1, 7)
    x_got(0, 1)
    x_got(0, 2)
    ring(1, 8)
    select(1, 1)
    far_y1 = y_send(1, 1)
    x_got(0, 3)
    for p in (1, 2, 3):
        y1[p].wait_recv()
        x_first(1, p)
    far_y_got(0, far_y0)
    for load in loads[4:]:
        load.wait()
    forward(0, 1)
    core0 = core_send(0)
    forward(0, 0)
    x_got(1, 0)
    x_got(1, 1)
    x0 = x_return_first(0, core0)
    x_got(1, 2)
    x_got(1, 3)
    far_y_got(1, far_y1)
    forward(1, 1)
    core1 = core_send(1)
    forward(1, 0)
    x1 = x_return_first(1, core1)
    x0 = x_return_second(0, *x0)
    x1 = x_return_second(1, *x1)
    back0 = y_return(0, core0, x0)
    some_grads(1)
    unselect(0, back0)

    z_sum = {}

    def z_back(place, block, device, into, number):
        zs[POS[place]] = block.astype(bf16)
        z_sum[place] = copy(zs.at[POS[place]], into.at[number], device)

    def z_odd(k):
        z_back(-k, zp[POS[-k]], z_dn, zr_m1, (7 - k) // 2)
        z_back(k, zp[POS[k]], z_up, zr_p1, (7 - k) // 2)

    def z_even(k):
        number = (8 - k) // 2
        block = zp[POS[-k]]
        if k < 8:
            z_sum[-k - 2].wait_recv()
            z_sum[-k - 1].wait_recv()
            block = block + zr_m2[number - 1].astype(f32) + zr_m1[number - 1].astype(f32)
        z_back(-k, block, z_dn2, zr_m2, number)
        if k < 8:
            z_sum[k + 1].wait_recv()
            block = zp[POS[k]] + zr_p1[number - 1].astype(f32)
            if k < 6:
                z_sum[k + 2].wait_recv()
                block = block + zr_p2[number - 1].astype(f32)
            z_back(k, block, z_up2, zr_p2, number)

    z_odd(3)
    z_odd(1)
    some_grads(1)
    back1 = y_return(1, core1, x1)
    some_grads(3)
    unselect(1, back1)
    z_even(8)
    z_odd(7)
    z_odd(5)
    some_grads(2)
    z_even(6)
    some_grads(2)
    z_even(4)
    some_grads(2)
    z_even(2)
    some_grads(len(tiles))
    total = zp[0]
    for place, got in ((-1, zr_m1), (1, zr_p1), (-2, zr_m2), (2, zr_p2)):
        z_sum[place].wait_recv()
        total = total + got[3].astype(f32)
    tg_ref[:, 0:HALF] = total[0:8].astype(bf16)
    tg_ref[:, HALF:D] = total[8:16].astype(bf16)
    store(tg_ref, tg_hbm)
    for one in stores:
        one.wait()

    for made in started:
        made.wait_send()


def deliver(*refs):
    ins, outs, held, sems = refs[0:4], refs[4:8], refs[8:12], refs[12]
    fetch = [pltpu.make_async_copy(ins[i], held[i], sems.at[0, i]) for i in range(4)]
    store = [pltpu.make_async_copy(held[i], outs[i], sems.at[1, i]) for i in range(4)]
    for one in fetch:
        one.start()
    for i in range(4):
        fetch[i].wait()
        store[i].start()
    for one in store:
        one.wait()


def body(tokens, cotangent, expert_ids, gate_codes, w_gate, w_up, w_down):
    hbm = pl.BlockSpec(memory_space=pl.ANY)
    shapes = (
        jax.ShapeDtypeStruct((8, D), bf16),
        jax.ShapeDtypeStruct((1, H, D), bf16),
        jax.ShapeDtypeStruct((1, H, D), bf16),
        jax.ShapeDtypeStruct((1, H, D), bf16),
    )
    results = pl.pallas_call(
        kernel,
        out_shape=shapes,
        in_specs=[hbm] * 7,
        out_specs=(hbm,) * 4,
        scratch_shapes=[pltpu.VMEM((8, D), bf16)] * 2
        + [pltpu.VMEM((8, 8), jnp.int32)] * 2
        + [pltpu.VMEM((H, D), bf16)] * 3
        + [
            pltpu.VMEM((NZ, 16, D + META), bf16),
            pltpu.VMEM((NZ, 16, D + META), bf16),
            pltpu.VMEM((2, 2, 3, PIECE, 2 * D), bf16),
            pltpu.VMEM((2, 128, 128), bf16),
            pltpu.VMEM((1024, 2 * D), bf16),
            pltpu.VMEM((H, 1024), bf16),
            pltpu.VMEM((H, 1024), bf16),
            pltpu.VMEM((H, 1024), bf16),
            pltpu.VMEM((2, 256, D), bf16),
            pltpu.VMEM((2, 256, D), bf16),
            pltpu.VMEM((2, 256, D), bf16),
        ]
        + [pltpu.VMEM((2, PLANE, D), bf16)] * 6
        + [
            pltpu.VMEM((2, 2, 3, PIECE, HALF), bf16),
            pltpu.VMEM((2, 2, 4, PIECE, HALF), bf16),
            pltpu.VMEM((NZ, 16, HALF), f32),
            pltpu.VMEM((NZ, 16, HALF), bf16),
        ]
        + [pltpu.VMEM((4, 16, HALF), bf16)] * 4
        + [pltpu.VMEM((8, D), bf16)]
        + [pltpu.VMEM((H, D), bf16)] * 3
        + [
            pltpu.SemaphoreType.DMA((COPIES,)),
            pltpu.SemaphoreType.DMA((COPIES,)),
            pltpu.SemaphoreType.DMA((7,)),
            pltpu.SemaphoreType.DMA((4,)),
        ],
        compiler_params=pltpu.CompilerParams(
            collective_id=0, has_side_effects=True, vmem_limit_bytes=60 * 1024 * 1024
        ),
        name="expert_layer_backward",
    )(tokens, cotangent, expert_ids, gate_codes, w_gate, w_up, w_down)
    return pl.pallas_call(
        deliver,
        out_shape=shapes,
        in_specs=[hbm] * 4,
        out_specs=(hbm,) * 4,
        scratch_shapes=[pltpu.VMEM(shape.shape, bf16) for shape in shapes]
        + [pltpu.SemaphoreType.DMA((2, 4))],
        compiler_params=pltpu.CompilerParams(vmem_limit_bytes=60 * 1024 * 1024),
        name="deliver",
    )(*results)


def solution(mesh):
    placed = (
        P(("dp", "expert"), None),
        P(("dp", "expert"), None),
        P(("dp", "expert"), None),
        P(("dp", "expert"), None),
        P("expert", "dp", None),
        P("expert", "dp", None),
        P("expert", "dp", None),
    )
    return jax.shard_map(
        body,
        mesh=mesh,
        in_specs=placed,
        out_specs=(
            P(("dp", "expert"), None),
            P("expert", "dp", None),
            P("expert", "dp", None),
            P("expert", "dp", None),
        ),
        check_vma=False,
    )
```

time: 132 us -> 109 us (0.83)
  the two profiles are of different devices: /device:TPU:8 before, /device:TPU:34 now
where the time goes in v3:
time: 109 us
  Pallas kernels  109 us (100%)
    pallas_call x1, Pallas kernels, body(): pl.pallas_call(kernel, out_shape=shapes, in_specs=[hbm] * 7, out_specs=(h...  106 us
    pallas_call x1, Pallas kernels, body(): pl.pallas_call(deliver, out_shape=shapes, in_specs=[hbm] * 4, out_specs=(...  2.62 us

profile of v3, /device:TPU:34, one launch (start us, length us, event | category | flops | bytes accessed | tf_op | source)
XLA Modules:
  0.0 109.3 jit_solution(12427501704084274660)
XLA Ops:
  0.6 105.9 %expert_layer_backward.1 = (bf16[8,2048]{1,0:T(8,128)(2,1)}, bf16[1,192,2048]{2,1,0:T(8,128)(2,1)}, bf16[1,192,2048]{2,1,0:T(8,128)(2,1)}, bf16[1,192,2048]{2,1,0:T(8,128)(2,1)}) custom-call(bf16[8,2048]{1,0:T(8,128)(2,1)} %tok_hbm.1, bf16[8,2048]{1,0:T(8,128)(2,1)} %cot_hbm.1, s32[8,8]{1,0:T(8,128)} %ids_hbm.1, s32[8,8]{1,0:T(8,128)} %codes_hbm.1, ...), custom_call_target="tpu_custom_call" | custom-call | tf_op jit(solution)/shard_map/expert_layer_backward/pallas_call | solution.py:433
  106.5 2.6 %deliver.1 = (bf16[8,2048]{1,0:T(8,128)(2,1)}, bf16[1,192,2048]{2,1,0:T(8,128)(2,1)}, bf16[1,192,2048]{2,1,0:T(8,128)(2,1)}, bf16[1,192,2048]{2,1,0:T(8,128)(2,1)}) custom-call(bf16[8,2048]{1,0:T(8,128)(2,1)} %get-tuple-element.8.refs_0_, bf16[1,192,2048]{2,1,0:T(8,128)(2,1)} %get-tuple-element.9.refs_1_, bf16[1,192,2048]{2,1,0:T(8,128)(2,1)} %get-tuple-element.10.refs_2_, ...), custom_call_target="tpu_custom_call" | custom-call | tf_op jit(solution)/shard_map/deliver/pallas_call | solution.py:475

commit v4 on v3

--- a/solution.py
+++ b/solution.py
@@ -17,8 +17,9 @@
 META = 128
 HALF = D // 2
 PIECE = 16
+TILE = 512
 PLANE = NY * PIECE
-COPIES = 192
+COPIES = 208
 
 OFFSETS = (0, -1, 1, -2, 2, -3, 3, -4, 4, -5, 5, -6, 6, -7, 7, -8)
 POS = {offset: place for place, offset in enumerate(OFFSETS)}
@@ -195,8 +196,7 @@
             for q in range(4):
                 for p in range(4):
                     sib[c, q, p].wait_recv()
-        first = base(c, 4 * half)
-        rows_here = pl.ds(first, 256)
+        rows_here = pl.ds(base(c, 4 * half), 256)
         pre_gate = dot_nt(xc[rows_here, 0:D], wg_ref[...])
         pre_up = dot_nt(xc[rows_here, 0:D], wu_ref[...])
         d_hidden = dot_nt(xc[rows_here, D:2 * D], wd_ref[...])
@@ -208,66 +208,113 @@
         h_t[:, rows_here] = hidden.T.astype(bf16)
         du_t[:, rows_here] = d_up.T.astype(bf16)
         dg_t[:, rows_here] = d_gate.T.astype(bf16)
-        d_up, d_gate = d_up.astype(bf16), d_gate.astype(bf16)
+        return d_gate.astype(bf16), d_up.astype(bf16)
+
+    def tile(j):
+        return pl.ds(TILE * j, TILE)
+
+    def forward_tile(c, half, d_gate, d_up, j):
         into = p_sib if half else p_own
-        for j in range(4):
-            cols = pl.ds(512 * j, 512)
-            part = dot(d_gate, wg_ref[:, cols]) + dot(d_up, wu_ref[:, cols])
-            into[c, :, cols] = part.astype(bf16)
-
-    def core_send(c):
-        return {
-            q: copy(p_sib.at[c, pl.ds(q * PLANE, PLANE)], p_got.at[c, pl.ds(q * PLANE, PLANE)], sibling)
-            for q in (3, 2, 1, 0)
-        }
-
-    def pair(c, q, cols):
+        part = dot(d_gate, wg_ref[:, tile(j)]) + dot(d_up, wu_ref[:, tile(j)])
+        into[c, :, tile(j)] = part.astype(bf16)
+
+    core = {}
+
+    def forward_sibling(c):
+        d_gate, d_up = forward(c, 1)
+        for j in (0, 2, 1, 3):
+            forward_tile(c, 1, d_gate, d_up, j)
+            core[c, j] = copy(p_sib.at[c, :, tile(j)], p_got.at[c, :, tile(j)], sibling)
+
+    def pair(c, q, j):
         here = pl.ds(q * PLANE, PLANE)
-        return p_own[c, here, cols].astype(f32) + p_got[c, here, cols].astype(f32)
-
-    left, right, both = pl.ds(0, HALF), pl.ds(HALF, HALF), pl.ds(0, D)
-
-    def x_return_first(c, core_copies):
-        core_copies[3].wait_recv()
-        xs_o[c] = pair(c, 3, both).astype(bf16)
-        relay_r = copy(xs_o.at[c, :, left], xr_o.at[c, :, left], x_up)
-        relay_l = copy(xs_o.at[c, :, right], xr_o.at[c, :, right], x_dn)
-        core_copies[2].wait_recv()
-        xs_r[c, :, right] = pair(c, 2, right).astype(bf16)
-        r_plain = copy(xs_r.at[c, :, right], xr_l.at[c, :, right], x_up)
-        core_copies[1].wait_recv()
-        xs_l[c, :, left] = pair(c, 1, left).astype(bf16)
-        l_plain = copy(xs_l.at[c, :, left], xr_r.at[c, :, left], x_dn)
-        return relay_r, relay_l, r_plain, l_plain
-
-    def x_return_second(c, relay_r, relay_l, r_plain, l_plain):
+        return p_own[c, here, tile(j)].astype(f32) + p_got[c, here, tile(j)].astype(f32)
+
+    back_x = {}
+
+    def x_return_first(c, g):
+        left, right = g, 2 + g
+        core[c, left].wait_recv()
+        xs_o[c, :, tile(left)] = pair(c, 3, left).astype(bf16)
+        relay_r = copy(xs_o.at[c, :, tile(left)], xr_o.at[c, :, tile(left)], x_up)
+        xs_l[c, :, tile(left)] = pair(c, 1, left).astype(bf16)
+        l_plain = copy(xs_l.at[c, :, tile(left)], xr_r.at[c, :, tile(left)], x_dn)
+        core[c, right].wait_recv()
+        xs_o[c, :, tile(right)] = pair(c, 3, right).astype(bf16)
+        relay_l = copy(xs_o.at[c, :, tile(right)], xr_o.at[c, :, tile(right)], x_dn)
+        xs_r[c, :, tile(right)] = pair(c, 2, right).astype(bf16)
+        r_plain = copy(xs_r.at[c, :, tile(right)], xr_l.at[c, :, tile(right)], x_up)
+        back_x[c, g] = [relay_r, relay_l, l_plain, r_plain]
+
+    def x_return_second(c, g):
+        left, right = g, 2 + g
+        relay_r, relay_l, l_plain, r_plain = back_x[c, g]
         relay_r.wait_recv()
-        xs_r[c, :, left] = (pair(c, 2, left) + xr_o[c, :, left].astype(f32)).astype(bf16)
-        r_sum = copy(xs_r.at[c, :, left], xr_l.at[c, :, left], x_up)
+        xs_r[c, :, tile(left)] = (pair(c, 2, left) + xr_o[c, :, tile(left)].astype(f32)).astype(bf16)
+        r_sum = copy(xs_r.at[c, :, tile(left)], xr_l.at[c, :, tile(left)], x_up)
         relay_l.wait_recv()
-        xs_l[c, :, right] = (pair(c, 1, right) + xr_o[c, :, right].astype(f32)).astype(bf16)
-        l_sum = copy(xs_l.at[c, :, right], xr_r.at[c, :, right], x_dn)
-        return r_plain, l_plain, r_sum, l_sum
-
-    def y_return(c, core_copies, arriving):
-        core_copies[0].wait_recv()
-        for one in arriving:
+        xs_l[c, :, tile(right)] = (pair(c, 1, right) + xr_o[c, :, tile(right)].astype(f32)).astype(bf16)
+        l_sum = copy(xs_l.at[c, :, tile(right)], xr_r.at[c, :, tile(right)], x_dn)
+        back_x[c, g] = [l_plain, r_plain, r_sum, l_sum]
+
+    back_y = {}
+
+    def y_return(c, g):
+        for one in back_x[c, g]:
             one.wait_recv()
-        sends = {}
-        for side, cols in enumerate((left, right)):
-            total = pair(c, 0, cols) + xr_l[c, :, cols].astype(f32) + xr_r[c, :, cols].astype(f32)
+        for side in range(2):
+            j = 2 * side + g
+            total = pair(c, 0, j) + xr_l[c, :, tile(j)].astype(f32) + xr_r[c, :, tile(j)].astype(f32)
             total = total.astype(bf16)
-            yr[c, side, 0] = total[0:PIECE]
-            ys[c, side] = total[PIECE:].reshape(3, PIECE, HALF)
+            yr[c, side, 0, :, tile(g)] = total[0:PIECE]
+            ys[c, side, :, :, tile(g)] = total[PIECE:].reshape(3, PIECE, TILE)
         for p in (3, 1, 2):
-            sends[p] = copy(ys.at[c, :, p - 1], yr.at[c, :, p], y_back[p])
-        return sends
-
-    def unselect(c, y_copies):
+            back_y[c, g, p] = copy(
+                ys.at[c, :, p - 1, :, tile(g)], yr.at[c, :, p, :, tile(g)], y_back[p]
+            )
+
+    def unselect(c, g):
         for p in (1, 2, 3):
-            y_copies[p].wait_recv()
-        part = dot(unsel[c], yr[c].reshape(128, HALF))
-        zp[8 * c:8 * c + 8] = part.reshape(8, 16, HALF)
+            back_y[c, g, p].wait_recv()
+        part = dot(unsel[c], yr[c, :, :, :, tile(g)].reshape(128, TILE))
+        zp[8 * c:8 * c + 8, :, tile(g)] = part.reshape(8, 16, TILE)
+
+    z_sum = {}
+
+    def z_back(place, g, block, device, into, number):
+        zs[POS[place], :, tile(g)] = block.astype(bf16)
+        z_sum[place, g] = copy(
+            zs.at[POS[place], :, tile(g)], into.at[number, :, tile(g)], device
+        )
+
+    def z_odd(k, g):
+        z_back(-k, g, zp[POS[-k], :, tile(g)], z_dn, zr_m1, (7 - k) // 2)
+        z_back(k, g, zp[POS[k], :, tile(g)], z_up, zr_p1, (7 - k) // 2)
+
+    def z_even(k, g):
+        number = (8 - k) // 2
+        block = zp[POS[-k], :, tile(g)]
+        if k < 8:
+            z_sum[-k - 2, g].wait_recv()
+            z_sum[-k - 1, g].wait_recv()
+            block = block + zr_m2[number - 1, :, tile(g)].astype(f32)
+            block = block + zr_m1[number - 1, :, tile(g)].astype(f32)
+        z_back(-k, g, block, z_dn2, zr_m2, number)
+        if k < 8:
+            z_sum[k + 1, g].wait_recv()
+            block = zp[POS[k], :, tile(g)] + zr_p1[number - 1, :, tile(g)].astype(f32)
+            if k < 6:
+                z_sum[k + 2, g].wait_recv()
+                block = block + zr_p2[number - 1, :, tile(g)].astype(f32)
+            z_back(k, g, block, z_up2, zr_p2, number)
+
+    def z_last(g):
+        total = zp[0, :, tile(g)]
+        for place, got in ((-1, zr_m1), (1, zr_p1), (-2, zr_m2), (2, zr_p2)):
+            z_sum[place, g].wait_recv()
+            total = total + got[3, :, tile(g)].astype(f32)
+        tg_ref[:, tile(g)] = total[0:8].astype(bf16)
+        tg_ref[:, tile(2 + g)] = total[8:16].astype(bf16)
 
     stores = []
 
@@ -315,92 +362,74 @@
     y0[3].wait_recv()
     x_first(0, 3)
     ring(0, 7)
+    x_got(0, 0)
     ring(1, 6)
-    x_got(0, 0)
+    x_got(0, 1)
     ring(0, 8)
     select(1, 0)
     y1 = y_send(1, 0)
     x_first(1, 0)
     ring(1, 7)
-    x_got(0, 1)
+    far_y_got(0, far_y0)
     x_got(0, 2)
+    x_got(0, 3)
+    for load in loads[4:]:
+        load.wait()
+    own0 = forward(0, 0)
     ring(1, 8)
     select(1, 1)
     far_y1 = y_send(1, 1)
-    x_got(0, 3)
-    for p in (1, 2, 3):
+    for p in (1, 2):
         y1[p].wait_recv()
         x_first(1, p)
-    far_y_got(0, far_y0)
-    for load in loads[4:]:
-        load.wait()
-    forward(0, 1)
-    core0 = core_send(0)
-    forward(0, 0)
+    forward_sibling(0)
+    y1[3].wait_recv()
+    x_first(1, 3)
+    for j in (0, 2, 1, 3):
+        forward_tile(0, 0, *own0, j)
     x_got(1, 0)
+    x_return_first(0, 0)
+    x_return_first(0, 1)
     x_got(1, 1)
-    x0 = x_return_first(0, core0)
     x_got(1, 2)
     x_got(1, 3)
     far_y_got(1, far_y1)
-    forward(1, 1)
-    core1 = core_send(1)
-    forward(1, 0)
-    x1 = x_return_first(1, core1)
-    x0 = x_return_second(0, *x0)
-    x1 = x_return_second(1, *x1)
-    back0 = y_return(0, core0, x0)
+
+    forward_sibling(1)
+    own1 = forward(1, 0)
+    forward_tile(1, 0, *own1, 0)
+    forward_tile(1, 0, *own1, 2)
+    x_return_first(1, 0)
+    forward_tile(1, 0, *own1, 1)
+    forward_tile(1, 0, *own1, 3)
+    x_return_first(1, 1)
+    x_return_second(0, 0)
+    x_return_second(0, 1)
+    x_return_second(1, 0)
+    x_return_second(1, 1)
+    y_return(0, 0)
+    y_return(0, 1)
     some_grads(1)
-    unselect(0, back0)
-
-    z_sum = {}
-
-    def z_back(place, block, device, into, number):
-        zs[POS[place]] = block.astype(bf16)
-        z_sum[place] = copy(zs.at[POS[place]], into.at[number], device)
-
-    def z_odd(k):
-        z_back(-k, zp[POS[-k]], z_dn, zr_m1, (7 - k) // 2)
-        z_back(k, zp[POS[k]], z_up, zr_p1, (7 - k) // 2)
-
-    def z_even(k):
-        number = (8 - k) // 2
-        block = zp[POS[-k]]
-        if k < 8:
-            z_sum[-k - 2].wait_recv()
-            z_sum[-k - 1].wait_recv()
-            block = block + zr_m2[number - 1].astype(f32) + zr_m1[number - 1].astype(f32)
-        z_back(-k, block, z_dn2, zr_m2, number)
-        if k < 8:
-            z_sum[k + 1].wait_recv()
-            block = zp[POS[k]] + zr_p1[number - 1].astype(f32)
-            if k < 6:
-                z_sum[k + 2].wait_recv()
-                block = block + zr_p2[number - 1].astype(f32)
-            z_back(k, block, z_up2, zr_p2, number)
-
-    z_odd(3)
-    z_odd(1)
+    y_return(1, 0)
+    y_return(1, 1)
+    for g in range(2):
+        unselect(0, g)
+        z_odd(3, g)
+        z_odd(1, g)
     some_grads(1)
-    back1 = y_return(1, core1, x1)
-    some_grads(3)
-    unselect(1, back1)
-    z_even(8)
-    z_odd(7)
-    z_odd(5)
-    some_grads(2)
-    z_even(6)
-    some_grads(2)
-    z_even(4)
-    some_grads(2)
-    z_even(2)
+    for g in range(2):
+        unselect(1, g)
+        z_even(8, g)
+        z_odd(7, g)
+        z_odd(5, g)
+        some_grads(1)
+    for k in (6, 4, 2):
+        for g in range(2):
+            z_even(k, g)
+            some_grads(1)
     some_grads(len(tiles))
-    total = zp[0]
-    for place, got in ((-1, zr_m1), (1, zr_p1), (-2, zr_m2), (2, zr_p2)):
-        z_sum[place].wait_recv()
-        total = total + got[3].astype(f32)
-    tg_ref[:, 0:HALF] = total[0:8].astype(bf16)
-    tg_ref[:, HALF:D] = total[8:16].astype(bf16)
+    for g in range(2):
+        z_last(g)
     store(tg_ref, tg_hbm)
     for one in stores:
         one.wait()

time: 109 us -> 104 us (0.954)
  the two profiles are of different devices: /device:TPU:34 before, /device:TPU:1 now
where the time goes in v4:
time: 104 us
  Pallas kernels  103 us (99%)
    pallas_call x1, Pallas kernels, body(): pl.pallas_call(kernel, out_shape=shapes, in_specs=[hbm] * 7, out_specs=(h...  100 us
    pallas_call x1, Pallas kernels, body(): pl.pallas_call(deliver, out_shape=shapes, in_specs=[hbm] * 4, out_specs=(...  2.62 us

profile of v4, /device:TPU:1, one launch (start us, length us, event | category | flops | bytes accessed | tf_op | source)
XLA Modules:
  0.0 103.8 jit_solution(11377455238843615590)
XLA Ops:
  0.6 100.4 %expert_layer_backward.1 = (bf16[8,2048]{1,0:T(8,128)(2,1)}, bf16[1,192,2048]{2,1,0:T(8,128)(2,1)}, bf16[1,192,2048]{2,1,0:T(8,128)(2,1)}, bf16[1,192,2048]{2,1,0:T(8,128)(2,1)}) custom-call(bf16[8,2048]{1,0:T(8,128)(2,1)} %tok_hbm.1, bf16[8,2048]{1,0:T(8,128)(2,1)} %cot_hbm.1, s32[8,8]{1,0:T(8,128)} %ids_hbm.1, s32[8,8]{1,0:T(8,128)} %codes_hbm.1, ...), custom_call_target="tpu_custom_call" | custom-call | tf_op jit(solution)/shard_map/expert_layer_backward/pallas_call | solution.py:462
  101.0 2.6 %deliver.1 = (bf16[8,2048]{1,0:T(8,128)(2,1)}, bf16[1,192,2048]{2,1,0:T(8,128)(2,1)}, bf16[1,192,2048]{2,1,0:T(8,128)(2,1)}, bf16[1,192,2048]{2,1,0:T(8,128)(2,1)}) custom-call(bf16[8,2048]{1,0:T(8,128)(2,1)} %get-tuple-element.8.refs_0_, bf16[1,192,2048]{2,1,0:T(8,128)(2,1)} %get-tuple-element.9.refs_1_, bf16[1,192,2048]{2,1,0:T(8,128)(2,1)} %get-tuple-element.10.refs_2_, ...), custom_call_target="tpu_custom_call" | custom-call | tf_op jit(solution)/shard_map/deliver/pallas_call | solution.py:504

commit v5 on v4

--- a/solution.py
+++ b/solution.py
@@ -335,8 +335,8 @@
         for _ in range(min(count, len(tiles))):
             grad_tile(*tiles.pop(0))
 
+    raw = copy(gz.at[0], gz_far.at[0], x_far)
     ring(0, 0)
-    raw = copy(gz.at[0], gz_far.at[0], x_far)
     ring(0, 1)
     raw.wait_recv()
     ring(1, 0)

time: 104 us -> 104 us (level)
  no operation moved by 1% of the time
where the time goes in v5:
time: 104 us
  Pallas kernels  103 us (99%)
    pallas_call x1, Pallas kernels, body(): pl.pallas_call(kernel, out_shape=shapes, in_specs=[hbm] * 7, out_specs=(h...  101 us
    pallas_call x1, Pallas kernels, body(): pl.pallas_call(deliver, out_shape=shapes, in_specs=[hbm] * 4, out_specs=(...  2.62 us

profile of v5, /device:TPU:1, one launch (start us, length us, event | category | flops | bytes accessed | tf_op | source)
XLA Modules:
  0.0 104.1 jit_solution(10016497270314447231)
XLA Ops:
  0.6 100.7 %expert_layer_backward.1 = (bf16[8,2048]{1,0:T(8,128)(2,1)}, bf16[1,192,2048]{2,1,0:T(8,128)(2,1)}, bf16[1,192,2048]{2,1,0:T(8,128)(2,1)}, bf16[1,192,2048]{2,1,0:T(8,128)(2,1)}) custom-call(bf16[8,2048]{1,0:T(8,128)(2,1)} %tok_hbm.1, bf16[8,2048]{1,0:T(8,128)(2,1)} %cot_hbm.1, s32[8,8]{1,0:T(8,128)} %ids_hbm.1, s32[8,8]{1,0:T(8,128)} %codes_hbm.1, ...), custom_call_target="tpu_custom_call" | custom-call | tf_op jit(solution)/shard_map/expert_layer_backward/pallas_call | solution.py:462
  101.4 2.6 %deliver.1 = (bf16[8,2048]{1,0:T(8,128)(2,1)}, bf16[1,192,2048]{2,1,0:T(8,128)(2,1)}, bf16[1,192,2048]{2,1,0:T(8,128)(2,1)}, bf16[1,192,2048]{2,1,0:T(8,128)(2,1)}) custom-call(bf16[8,2048]{1,0:T(8,128)(2,1)} %get-tuple-element.8.refs_0_, bf16[1,192,2048]{2,1,0:T(8,128)(2,1)} %get-tuple-element.9.refs_1_, bf16[1,192,2048]{2,1,0:T(8,128)(2,1)} %get-tuple-element.10.refs_2_, ...), custom_call_target="tpu_custom_call" | custom-call | tf_op jit(solution)/shard_map/deliver/pallas_call | solution.py:504
